TPU v7x, 512 devices: a whole 4x4x16 slice. The times are simulated.
512 devices in a mesh: roll: 64 (over y, z_lo, x), learn: 8 (over z_hi, core).
Axes of the slice: x: 4, y: 4, z: 16 (z_hi: 4, z_lo: 4; z = z_hi * 4 + z_lo), core: 2. Of those that a mesh axis runs over, the one named last changes fastest.
Arguments:
- x_rows: bfloat16 [3, 1024, 5120], P(None, 'roll'), may hold values from -6 to 6
- query_base_rows: bfloat16 [3, 1024, 5120], P(None, 'roll', 'learn'), may hold values from -8 to 8
- k_base: bfloat16 [3, 1024, 1024], P(None, 'roll', 'learn'), may hold values from -6 to 6
- value_base_rows: bfloat16 [3, 1024, 1024], P(None, 'roll', 'learn'), may hold values from -6 to 6
- k_pool: bfloat16 [2048, 128, 1024], P('roll', None, 'learn'), may hold values from -8 to 8
- v_pool: bfloat16 [2048, 128, 1024], P('roll', None, 'learn'), may hold values from -6 to 6
- block_dest: int32 [2048, 1], P('roll'), may hold values from 0 to 63; in each aligned block of 32 rows (0 to 31, 32 to 63, ...) no two rows name the same one
- block_slot: int32 [2048], P('roll'), may hold values from 0 to 15
- block_fill: int32 [2048], P('roll'), may hold values from 2 to 128, as said below
- a_query: bfloat16 [5120, 64], P('learn'), may hold values from -0.078125 to 0.078125
- query_up_factor: bfloat16 [64, 5120], P(None, 'learn'), may hold values from -0.75 to 0.75
- a_value: bfloat16 [5120, 64], P('learn'), may hold values from -0.078125 to 0.078125
- value_up_factor: bfloat16 [64, 1024], P(None, 'learn'), may hold values from -0.75 to 0.75
Outputs:
- attended: bfloat16 [3, 1024, 5120], P(None, 'roll', 'learn')
Inputs may be any that keep to these rules, and one draw needn't show every extreme that they name: `block_dest`: within the 32 blocks of one index of roll at most 1 have the same owner, and some owner gets exactly 1 of them. `block_fill`: the live tokens of a block are its first ones; some block of every index of roll is full.
All inputs are finite; a program needn't handle non-finite values.
Results may differ from a plain program's by a relative error of at most 0.0051.
Values may be sent and summed in bfloat16 or wider, within the bound.
A program may use at most 64 MiB of HBM per device.

v0:
```python
import math

import jax
import jax.numpy as jnp
from jax import lax
from jax.sharding import PartitionSpec as P

HD = 128


adapter_scale = 0.5
masked_score = -1e30


def block_partials(queries, keys, values, fill):
    scores = jnp.einsum(
        "nkqd,njkd->nkqj", queries, keys, preferred_element_type=jnp.float32
    ) / math.sqrt(queries.shape[-1])
    live = (
        jnp.arange(keys.shape[1], dtype=jnp.int32)[None, None, None, :] < fill[:, None, None, None]
    )
    scores = jnp.where(live, scores, masked_score)
    peak = jnp.max(scores, axis=3)
    weights = jnp.where(live, jnp.exp(scores - peak[..., None]), 0.0)
    total = jnp.sum(weights, axis=3)
    mixed = jnp.einsum(
        "nkqj,njkd->nkqd", weights.astype(jnp.bfloat16), values, preferred_element_type=jnp.float32
    )
    return (peak, total, mixed)


def new_partials(queries, keys, values, steps, group):
    scores = jnp.einsum(
        "skqd,uskd->skqu", queries, keys, preferred_element_type=jnp.float32
    ) / math.sqrt(queries.shape[-1])
    row_step = jnp.arange(steps * group, dtype=jnp.int32) // group
    live = jnp.arange(steps, dtype=jnp.int32)[None, :] <= row_step[:, None]
    scores = jnp.where(live[None, None], scores, masked_score)
    peak = jnp.max(scores, axis=3)
    weights = jnp.where(live[None, None], jnp.exp(scores - peak[..., None]), 0.0)
    total = jnp.sum(weights, axis=3)
    mixed = jnp.einsum(
        "skqu,uskd->skqd", weights.astype(jnp.bfloat16), values, preferred_element_type=jnp.float32
    )
    return (peak, total, mixed)


def on_device(
    x_rows,
    query_base_rows,
    k_base,
    value_base_rows,
    k_pool,
    v_pool,
    block_dest,
    block_slot,
    block_fill,
    a_query,
    query_up_factor,
    a_value,
    value_up_factor,
):
    peers = lax.axis_size("roll")
    steps, slots, width = x_rows.shape
    pool = k_pool.shape[0]
    per_dest = max(1, 2 * pool // peers)
    lanes = peers * per_dest
    block_len = k_pool.shape[1]
    kv_local = k_pool.shape[2] // HD
    group = query_up_factor.shape[1] // (kv_local * HD)
    target = block_dest[:, 0]
    target_hot = (target[:, None] == jnp.arange(peers, dtype=jnp.int32)[None, :]).astype(jnp.int32)
    earlier = jnp.cumsum(target_hot, axis=0) - target_hot
    lane_of = target * per_dest + jnp.sum(earlier * target_hot, axis=1)
    placed = (lane_of[:, None] == jnp.arange(lanes, dtype=jnp.int32)[None, :]).astype(jnp.int32)
    occupied = jnp.sum(placed, axis=0) > 0
    source_of = jnp.sum(placed * jnp.arange(pool, dtype=jnp.int32)[:, None], axis=0)
    tags = jnp.stack([block_slot, block_fill], axis=1)
    sent_tags = jnp.where(occupied[:, None], tags[source_of], 0)
    got_tags = lax.all_to_all(sent_tags, "roll", split_axis=0, concat_axis=0, tiled=True)
    lane_slot = got_tags[:, 0]
    lane_fill = got_tags[:, 1]
    lane_live = lane_fill > 0
    flat = x_rows.reshape(steps * slots, width)
    query_down_product = jnp.dot(
        flat,
        lax.all_gather(a_query, "learn", axis=0, tiled=True),
        preferred_element_type=jnp.float32,
    )
    value_down_product = jnp.dot(
        flat,
        lax.all_gather(a_value, "learn", axis=0, tiled=True),
        preferred_element_type=jnp.float32,
    )
    query_vectors = query_base_rows.astype(jnp.float32) + adapter_scale * jnp.dot(
        query_down_product.astype(jnp.bfloat16), query_up_factor, preferred_element_type=jnp.float32
    ).reshape(query_base_rows.shape)
    query_vectors = query_vectors.astype(jnp.bfloat16)
    fresh_value_rows = value_base_rows.astype(jnp.float32) + adapter_scale * jnp.dot(
        value_down_product.astype(jnp.bfloat16), value_up_factor, preferred_element_type=jnp.float32
    ).reshape(value_base_rows.shape)
    fresh_value_rows = fresh_value_rows.astype(jnp.bfloat16)
    q_slot = (
        query_vectors.reshape(steps, slots, kv_local, group, HD)
        .transpose(1, 2, 0, 3, 4)
        .reshape(slots, kv_local, steps * group, HD)
    )
    key_new = k_base.reshape(steps, slots, kv_local, HD)
    value_rows = fresh_value_rows.reshape(steps, slots, kv_local, HD)
    peak_new, total_new, mixed_new = new_partials(q_slot, key_new, value_rows, steps, group)
    sent_keys = jnp.where(occupied[:, None, None], k_pool[source_of], jnp.zeros((), jnp.bfloat16))
    sent_values = jnp.where(occupied[:, None, None], v_pool[source_of], jnp.zeros((), jnp.bfloat16))
    got_keys, got_values = (
        lax.all_to_all(sent_keys, "roll", split_axis=0, concat_axis=0, tiled=True),
        lax.all_to_all(sent_values, "roll", split_axis=0, concat_axis=0, tiled=True),
    )
    lane_shape = (lanes, block_len, kv_local, HD)
    peak, total, mixed = block_partials(
        q_slot[lane_slot], got_keys.reshape(lane_shape), got_values.reshape(lane_shape), lane_fill
    )
    peak = jnp.where(lane_live[:, None, None], peak, masked_score)
    member = (lane_slot[:, None] == jnp.arange(slots, dtype=jnp.int32)[None, :]) & lane_live[
        :, None
    ]
    block_peak = jnp.max(jnp.where(member[:, :, None, None], peak[:, None], masked_score), axis=0)
    top = jnp.maximum(block_peak, peak_new)
    lane_weight = jnp.where(lane_live[:, None, None], jnp.exp(peak - top[lane_slot]), 0.0)
    member_weight = member.astype(jnp.float32)
    total_all = total_new * jnp.exp(peak_new - top) + jnp.einsum(
        "ls,lkq->skq", member_weight, lane_weight * total, precision=lax.Precision.HIGHEST
    )
    mixed_all = mixed_new * jnp.exp(peak_new - top)[..., None] + jnp.einsum(
        "ls,lkqd->skqd",
        member_weight,
        lane_weight[..., None] * mixed,
        precision=lax.Precision.HIGHEST,
    )
    result = mixed_all / total_all[..., None]
    result = (
        result.reshape(slots, kv_local, steps, group, HD)
        .transpose(2, 0, 1, 3, 4)
        .reshape(steps, slots, kv_local * group * HD)
    )
    return result.astype(jnp.bfloat16)


def solution(mesh):
    return jax.shard_map(
        on_device,
        mesh=mesh,
        in_specs=(
            P(None, "roll", None),
            P(None, "roll", "learn"),
            P(None, "roll", "learn"),
            P(None, "roll", "learn"),
            P("roll", None, "learn"),
            P("roll", None, "learn"),
            P("roll", None),
            P("roll"),
            P("roll"),
            P("learn", None),
            P(None, "learn"),
            P("learn", None),
            P(None, "learn"),
        ),
        out_specs=P(None, "roll", "learn"),
        check_vma=False,
    )
```

profile of v0, /device:TPU:65, one launch (start us, length us, event | category | flops | bytes accessed | tf_op | source)
XLA Modules:
  0.0 201.6 jit_solution(5350927864130700451)
XLA Ops:
  0.0 0.0 copy-start
  0.0 0.8 fusion.19
  0.8 0.1 reduce_window_sum.11
  0.9 0.8 select_reduce_fusion.2
  1.7 0.7 fusion.27
  2.4 0.1 convert_reduce_fusion
  2.5 0.7 pad_add_fusion
  3.2 0.1 copy.68
  3.3 0.6 gather_fusion
  3.9 0.1 copy.69
  3.9 0.7 copy.70
  4.7 10.6 %all-to-all-start = ((s32[64,1,2]{2,1,0:T(1,128)}), s32[64,1,2]{2,1,0:T(1,128)S(1)}, u32[]{:S(2)}, u32[]{:S(2)}) async-start(s32[64,1,2]{2,1,0:T(1,128)} %copy.70), calls=%async_computation | async-start | bytes 65536 | tf_op jit(solution)/shard_map/all_to_all | solution.py:80
  15.3 0.0 copy-done
  15.3 0.0 copy-start.1
  15.3 2.1 %gather_fusion.2 = bf16[64,128,128]{2,1,0:T(8,128)(2,1)} fusion(bf16[32,128,128]{2,1,0:T(8,128)(2,1)S(1)} %copy-done, s32[1024]{0:T(1024)S(1)} %pad_clamp_fusion.1), kind=kCustom, calls=%fused_computation.2 | custom fusion | bytes 4194560 | tf_op jit(solution)/shard_map/gather | solution.py:111
  17.5 0.0 copy-done.1
  17.5 2.2 %gather_fusion.4 = bf16[64,128,128]{2,1,0:T(8,128)(2,1)} fusion(bf16[32,128,128]{2,1,0:T(8,128)(2,1)S(1)} %copy-done.1, s32[1024]{0:T(1024)S(1)} %pad_clamp_fusion.1), kind=kCustom, calls=%fused_computation.4 | custom fusion | bytes 4194560 | tf_op jit(solution)/shard_map/gather | solution.py:112
  19.6 3.9 %broadcast_select_fusion.1 = (bf16[64,128,128]{2,1,0:T(8,128)(2,1)S(1)}, bf16[64,128,128]{2,1,0:T(8,128)(2,1)}) fusion(bf16[64,128,128]{2,1,0:T(8,128)(2,1)} %gather_fusion.2, pred[64]{0:T(512)(128)(4,1)S(1)} %broadcast_compare_fusion.1, bf16[64,128,128]{2,1,0:T(8,128)(2,1)} %gather_fusion.4), kind=kLoop, calls=%fused_computation.6 | loop fusion | flops 2097152 | bytes 8388672 | tf_op jit(solution)/shard_map/jit(_where)/select_n | solution.py:111
  23.5 0.0 all-to-all-done
  23.5 58.4 %all_to_all.19 = bf16[64,128,128]{2,1,0:T(8,128)(2,1)} all-to-all(bf16[64,128,128]{2,1,0:T(8,128)(2,1)S(1)} %get-tuple-element.12), channel_id=1, replica_groups=mesh['roll'=64,'learn'=8] {'roll'}, dimensions={0} | all-to-all | bytes 4194304 | tf_op jit(solution)/shard_map/all_to_all | solution.py:114
  81.9 0.0 copy-start.2
  81.9 0.0 copy-start.3
  81.9 8.0 %all-to-all-start.2 = ((bf16[64,128,128]{2,1,0:T(8,128)(2,1)}), bf16[64,128,128]{2,1,0:T(8,128)(2,1)S(1)}, u32[]{:S(2)}, u32[]{:S(2)}) async-start(bf16[64,128,128]{2,1,0:T(8,128)(2,1)} %get-tuple-element.13), calls=%async_computation.2 | async-start | bytes 4194304 | tf_op jit(solution)/shard_map/all_to_all | solution.py:115
  89.9 0.0 copy-done.2
  90.0 0.0 copy-start.4
  90.0 74.2 %all_gather.6 = bf16[5120,64]{0,1:T(8,128)(2,1)} all-gather(bf16[640,64]{0,1:T(8,128)(2,1)S(1)} %copy-done.2), channel_id=1, replica_groups=mesh['roll'=64,'learn'=8] {'learn'}, dimensions={0}, use_global_device_ids=true | all-gather | bytes 737280 | tf_op jit(solution)/shard_map/all_gather | solution.py:87
  164.2 0.0 copy-done.3
  164.2 0.0 copy-start.7
  164.2 1.7 convolution_multiply_fusion.3
  165.9 0.8 add_convert_fusion
  166.8 0.1 reshape.361
  166.9 0.0 copy-start.9
  167.0 0.9 fusion.34
  167.8 0.0 copy-start.5
  167.9 0.0 copy-done.4
  167.9 21.0 %all_gather.7 = bf16[5120,64]{0,1:T(8,128)(2,1)} all-gather(bf16[640,64]{0,1:T(8,128)(2,1)S(1)} %copy-done.4), channel_id=1, replica_groups=mesh['roll'=64,'learn'=8] {'learn'}, dimensions={0}, use_global_device_ids=true | all-gather | bytes 737280 | tf_op jit(solution)/shard_map/all_gather | solution.py:92
  188.9 1.7 convolution_multiply_fusion.5
  190.6 0.0 copy-done.7
  190.6 0.6 add_convert_fusion.1
  191.2 0.1 copy.71
  191.3 0.0 copy-done.9
  191.3 0.0 copy-done.5
  191.3 0.6 gather_fusion.1
  192.0 0.1 iota_compare_fusion
  192.1 3.6 %fusion.33 = (f32[64,15]{1,0:T(8,128)S(1)}, f32[64,15,128]{2,1,0:T(8,128)}) fusion(bf16[64,15,128]{2,1,0:T(8,128)(2,1)S(1)} %gather_fusion.1, bf16[64,128,128]{2,1,0:T(8,128)(2,1)} %all_to_all.19, pred[64,128]{1,0:T(8,128)(4,1)S(1)} %iota_compare_fusion), kind=kOutput, calls=%fused_computation.77 | convolution fusion | flops 31824960 | bytes 2846464 | tf_op jit(solution)/shard_map/nkqd,njkd->nkqj/dot_general | solution.py:16
  195.7 0.1 broadcast_select_fusion.2
  195.7 0.1 copy.73
  195.8 0.1 select_reduce_fusion
  195.9 0.1 copy.74
  196.0 0.6 gather_fusion.3
  196.6 1.4 fusion.7
  198.1 0.0 copy-start.6
  198.1 0.0 copy-start.8
  198.1 0.0 copy-start.10
  198.1 0.1 exponential_select_fusion.1
  198.2 0.0 all-to-all-done.2
  198.2 1.8 convolution_multiply_fusion
  200.0 0.4 fusion.5
  200.4 0.1 convolution_add_fusion
  200.5 0.0 copy-done.6
  200.5 0.0 copy-done.8
  200.5 0.0 copy-done.10
  200.5 0.2 fusion.3
  200.8 0.7 convert_element_type.58
  (17 shorter events, 0.2 us)
Async XLA Ops:
  0.0 15.3 %copy-start = (bf16[32,128,128]{2,1,0:T(8,128)(2,1)S(1)}, bf16[32,128,128]{2,1,0:T(8,128)(2,1)}, u32[]{:S(2)}) copy-start(bf16[32,128,128]{2,1,0:T(8,128)(2,1)} %param.17) | copy-start | bytes 3145732
  4.7 18.8 %all-to-all-start = ((s32[64,1,2]{2,1,0:T(1,128)}), s32[64,1,2]{2,1,0:T(1,128)S(1)}, u32[]{:S(2)}, u32[]{:S(2)}) async-start(s32[64,1,2]{2,1,0:T(1,128)} %copy.70), calls=%async_computation | async-start | bytes 65536 | tf_op jit(solution)/shard_map/all_to_all | solution.py:80
  15.3 2.1 %copy-start.1 = (bf16[32,128,128]{2,1,0:T(8,128)(2,1)S(1)}, bf16[32,128,128]{2,1,0:T(8,128)(2,1)}, u32[]{:S(2)}) copy-start(bf16[32,128,128]{2,1,0:T(8,128)(2,1)} %param.18) | copy-start | bytes 3145732
  81.9 8.1 %copy-start.2 = (bf16[640,64]{0,1:T(8,128)(2,1)S(1)}, bf16[640,64]{0,1:T(8,128)(2,1)}, u32[]{:S(2)}) copy-start(bf16[640,64]{0,1:T(8,128)(2,1)} %param.22) | copy-start | bytes 245764
  81.9 82.3 %copy-start.3 = (bf16[64,640]{1,0:T(8,128)(2,1)S(1)}, bf16[64,640]{1,0:T(8,128)(2,1)}, u32[]{:S(2)}) copy-start(bf16[64,640]{1,0:T(8,128)(2,1)} %param.23) | copy-start | bytes 245764
  81.9 116.3 %all-to-all-start.2 = ((bf16[64,128,128]{2,1,0:T(8,128)(2,1)}), bf16[64,128,128]{2,1,0:T(8,128)(2,1)S(1)}, u32[]{:S(2)}, u32[]{:S(2)}) async-start(bf16[64,128,128]{2,1,0:T(8,128)(2,1)} %get-tuple-element.13), calls=%async_computation.2 | async-start | bytes 4194304 | tf_op jit(solution)/shard_map/all_to_all | solution.py:115
  90.0 77.9 %copy-start.4 = (bf16[640,64]{0,1:T(8,128)(2,1)S(1)}, bf16[640,64]{0,1:T(8,128)(2,1)}, u32[]{:S(2)}) copy-start(bf16[640,64]{0,1:T(8,128)(2,1)} %param.24) | copy-start | bytes 245764
  164.2 26.4 %copy-start.7 = (bf16[3,16,128]{2,1,0:T(8,128)(2,1)S(1)}, bf16[3,16,128]{2,1,0:T(8,128)(2,1)}, u32[]{:S(2)}) copy-start(bf16[3,16,128]{2,1,0:T(8,128)(2,1)} %param.16) | copy-start | bytes 36868
  166.9 24.4 %copy-start.9 = (pred[15,3]{0,1:T(4,128)(4,1)}, pred[15,3]{0,1:T(4,128)(4,1)S(1)}, u32[]{:S(2)}) copy-start(pred[15,3]{0,1:T(4,128)(4,1)S(1)} %iota_compare_fusion.4) | copy-start | bytes 139
  167.8 23.5 %copy-start.5 = (f32[16,15,3]{1,2,0:T(4,128)}, f32[16,15,3]{1,2,0:T(4,128)S(1)}, u32[]{:S(2)}) copy-start(f32[16,15,3]{1,2,0:T(4,128)S(1)} %get-tuple-element.17) | copy-start | bytes 8644
  198.1 2.4 %copy-start.6 = (f32[16,15,3]{1,2,0:T(4,128)S(1)}, f32[16,15,3]{1,2,0:T(4,128)}, u32[]{:S(2)}) copy-start(f32[16,15,3]{1,2,0:T(4,128)} %copy-done.5) | copy-start | bytes 8644
  198.1 2.4 %copy-start.8 = (bf16[3,16,128]{2,1,0:T(8,128)(2,1)S(1)}, bf16[3,16,128]{2,1,0:T(8,128)(2,1)}, u32[]{:S(2)}) copy-start(bf16[3,16,128]{2,1,0:T(8,128)(2,1)} %add_convert_fusion.1) | copy-start | bytes 36868
  198.1 2.4 %copy-start.10 = (pred[15,3]{0,1:T(4,128)(4,1)S(1)}, pred[15,3]{0,1:T(4,128)(4,1)}, u32[]{:S(2)}) copy-start(pred[15,3]{0,1:T(4,128)(4,1)} %copy-done.9) | copy-start | bytes 139
where the time goes:
time: 202 us
  blocking collectives  154 us (76%)
  starting transfers between devices  18.7 us (9%)
  matrix products  10.4 us (5%)
  other arithmetic  10.3 us (5%)
  local copies, waits for them, and re-layouts  8.17 us (4%)
    all_gather x1, blocking collectives, on_device(): lax.all_gather(a_query, 'learn', axis=0, tiled=True)  74.2 us
    all_to_all x1, blocking collectives, on_device(): lax.all_to_all(sent_keys, 'roll', split_axis=0, concat_axis=0, tiled=True)  58.4 us
    all_gather x1, blocking collectives, on_device(): lax.all_gather(a_value, 'learn', axis=0, tiled=True)  21 us
    all_to_all x1, starting transfers between devices, on_device(): lax.all_to_all(sent_tags, 'roll', split_axis=0, concat_axis=0, tiled=True)  10.6 us
    all_to_all x1, starting transfers between devices, on_device(): lax.all_to_all(sent_values, 'roll', split_axis=0, concat_axis=0, tiled=True)  8.04 us
  transfers between devices with their start and end apart: 2, of which 0 were waited for; matrix products, arithmetic and copies ran while one was open for 10% of the time, Pallas kernels for 0%

commit v1 on v0

v1 whole, which is shorter than its diff:
```python
import functools
import math

import jax
import jax.numpy as jnp
from jax import lax
from jax.experimental import pallas as pl
from jax.experimental.pallas import tpu as pltpu
from jax.sharding import PartitionSpec as P

MESH = pl.DeviceIdType.MESH
F32 = jnp.float32
BF16 = jnp.bfloat16
HD = 128
ROWS = 16
adapter_scale = 0.5
masked_score = -1e30
no_slot = -1000.0


def iota(shape, dim):
    return lax.broadcasted_iota(jnp.int32, shape, dim)


def diagonal(column):
    n = column.shape[0]
    here = iota((n, HD), 1) == lax.rem(iota((n, HD), 0), ROWS)
    spread = jnp.where(here, jnp.broadcast_to(column, (n, HD)), 0.0)
    return jnp.sum(spread.reshape(n // ROWS, ROWS, HD), axis=1)


def kernel(
    peers,
    ranks,
    dims,
    x_hbm,
    qb_hbm,
    kb_hbm,
    vb_hbm,
    kp_hbm,
    vp_hbm,
    dest,
    slot,
    fill,
    aq_hbm,
    qu_hbm,
    av_hbm,
    vu_hbm,
    out_ref,
    x,
    qb,
    kb,
    vb,
    kp,
    vp,
    aq,
    qu,
    av,
    vu,
    tag_send,
    tag_recv,
    lane_vec,
    lane_blk,
    lq_recv,
    lv_recv,
    tagc,
    sel,
    sel_t,
    q_send,
    q_recv,
    part,
    lse_blk,
    p_send,
    p_recv,
    l_send,
    l_recv,
    new_mixed,
    top_s,
    den_s,
    wide,
    weighted,
    local_sem,
    blk_sem,
    send_sem,
    recv_sem,
    low_send_sem,
    low_recv_sem,
):
    steps, slots, chunk, pool, block_len, group = dims
    rows = steps * group
    me, ml = lax.axis_index("roll"), lax.axis_index("learn")
    others = pl.ds(0, peers - 1)

    barrier = pltpu.get_barrier_semaphore()

    def greet(i, carry):
        pl.semaphore_signal(
            barrier, inc=1, device_id=(lax.rem(me + i, peers), ml), device_id_type=MESH
        )
        return carry

    lax.fori_loop(1, peers, greet, 0)
    for i in range(1, ranks):
        pl.semaphore_signal(
            barrier, inc=1, device_id=(me, lax.rem(ml + i, ranks)), device_id_type=MESH
        )

    start = pl.multiple_of(ml * chunk, HD)
    pairs = [
        (x_hbm.at[:, :, pl.ds(start, chunk)], x),
        (aq_hbm, aq),
        (av_hbm, av),
        (qb_hbm, qb),
        (qu_hbm, qu),
        (kb_hbm, kb),
        (vb_hbm, vb),
        (vu_hbm, vu),
        (kp_hbm, kp),
        (vp_hbm, vp),
    ]
    loads = [pltpu.make_async_copy(a, b, local_sem.at[i]) for i, (a, b) in enumerate(pairs)]
    for load in loads:
        load.start()

    lane = iota((1, HD), 1)
    tag_row = jnp.full((1, HD), no_slot, F32)
    blk_row = jnp.zeros((1, HD), jnp.int32)
    for b in range(pool):
        hit = lane == dest[b, 0]
        tag_row = jnp.where(hit, slot[b].astype(F32), tag_row)
        blk_row = jnp.where(hit, b, blk_row)
    tag_send[...] = tag_row
    tag_recv[pl.ds(me, 1), :] = tag_row
    lane_vec[...] = blk_row
    to_smem = pltpu.make_async_copy(lane_vec, lane_blk, blk_sem)
    to_smem.start()

    for load in loads[:3]:
        load.wait()
    x_rows = x[...].reshape(steps * slots, chunk)
    half = steps * slots // 2

    def packed(a):
        low = jnp.dot(x_rows, a[...], preferred_element_type=F32)
        return jnp.concatenate([low[:half], low[half:]], axis=1)

    lq_recv[ml] = packed(aq)
    lv_recv[ml] = packed(av)

    pl.semaphore_wait(barrier, peers + ranks - 2)

    def to_learn(buf, k):
        copies = []
        for i in range(1, ranks):
            copies.append(
                pltpu.make_async_remote_copy(
                    src_ref=buf.at[ml],
                    dst_ref=buf.at[ml],
                    send_sem=low_send_sem.at[k],
                    recv_sem=low_recv_sem.at[k],
                    device_id=(me, lax.rem(ml + i, ranks)),
                    device_id_type=MESH,
                )
            )
            copies[-1].start()

    to_learn(lq_recv, 0)

    def to_roll(src_of, dst, k):
        def one(i, carry):
            d = lax.rem(me + i, peers)
            pltpu.make_async_remote_copy(
                src_ref=src_of(d),
                dst_ref=dst,
                send_sem=send_sem.at[k],
                recv_sem=recv_sem.at[k],
                device_id=(d, ml),
                device_id_type=MESH,
            ).start()
            return carry

        lax.fori_loop(1, peers, one, 0)

    to_roll(lambda d: tag_send, tag_recv.at[pl.ds(me, 1), :], 0)
    to_learn(lv_recv, 1)

    def wait_lanes(buf, sem):
        pltpu.make_async_copy(buf.at[others], buf.at[others], sem).wait()

    def wait_learn(buf, sem):
        rest = buf.at[pl.ds(0, ranks - 1)]
        pltpu.make_async_copy(rest, rest, sem).wait()

    wait_lanes(tag_recv, recv_sem.at[0])
    mine = iota((peers, HD), 1) == me
    asked = jnp.sum(jnp.where(mine, tag_recv[...], 0.0), axis=1, keepdims=True)
    tagc[...] = jnp.broadcast_to(asked, (peers, HD))

    width = ROWS * slots
    sel_row = (iota((ROWS, width), 0) * slots).astype(F32)
    sel_lane = iota((ROWS, width), 1).astype(F32)

    def pick(l, carry):
        row = tagc[pl.ds(l, 1), :]
        want = sel_row + jnp.concatenate([row] * (width // HD), axis=1)
        hot = jnp.where(want == sel_lane, 1.0, 0.0).astype(BF16)
        sel[pl.ds(pl.multiple_of(l * ROWS, ROWS), ROWS), :] = hot
        return carry

    lax.fori_loop(0, peers, pick, 0, unroll=8)

    def unpacked(buf):
        low = buf[0]
        for i in range(1, ranks):
            low = low + buf[i]
        rank = low.shape[1] // 2
        return jnp.concatenate([low[:, :rank], low[:, rank:]], axis=0).astype(BF16)

    for load in loads[3:5]:
        load.wait()
    wait_learn(lq_recv, low_recv_sem.at[0])
    up = jnp.dot(unpacked(lq_recv), qu[...], preferred_element_type=F32)
    query = qb[...].reshape(steps * slots, group * HD).astype(F32) + adapter_scale * up
    query = query.astype(BF16)
    tiles = [
        query[t * slots : (t + 1) * slots, g * HD : (g + 1) * HD]
        for t in range(steps)
        for g in range(group)
    ]
    stack = jnp.concatenate(tiles + [jnp.zeros((slots, HD), BF16)] * (ROWS - rows), axis=0)
    picked = jnp.dot(sel[...], stack, preferred_element_type=F32).astype(BF16)
    q_send[...] = picked.reshape(peers, ROWS, HD)
    q_recv[me] = q_send[me]
    to_roll(lambda d: q_send.at[d], q_recv.at[me], 1)

    sel_t[...] = sel[...].T
    for load in loads[5:8]:
        load.wait()
    wait_learn(lv_recv, low_recv_sem.at[1])
    up_v = jnp.dot(unpacked(lv_recv), vu[...], preferred_element_type=F32)
    value = vb[...].reshape(steps * slots, HD).astype(F32) + adapter_scale * up_v
    value = value.astype(BF16).astype(F32)
    values = [value[t * slots : (t + 1) * slots] for t in range(steps)]
    keys = [kb[t].astype(F32) for t in range(steps)]
    scale = 1.0 / math.sqrt(HD)
    lane_s = iota((slots, HD), 1)
    scores = [jnp.full((slots, HD), masked_score, F32) for _ in range(steps)]
    for r in range(rows):
        q_r = tiles[r].astype(F32)
        for u in range(r // group + 1):
            s = jnp.sum(q_r * keys[u], axis=1, keepdims=True) * scale
            scores[u] = jnp.where(lane_s == r, s, scores[u])
    new_peak = functools.reduce(jnp.maximum, scores)
    new_w = [
        jnp.where(lane_s >= u * group, jnp.exp(scores[u] - new_peak), 0.0) for u in range(steps)
    ]
    new_total = functools.reduce(jnp.add, new_w)
    rounded = [w.astype(BF16).astype(F32) for w in new_w]
    for r in range(rows):
        acc = jnp.zeros((slots, HD), F32)
        for u in range(r // group + 1):
            acc = acc + rounded[u][:, r : r + 1] * values[u]
        new_mixed[pl.ds(r * slots, slots), :] = acc

    for load in loads[8:]:
        load.wait()
    to_smem.wait()
    wait_lanes(q_recv, recv_sem.at[1])
    batch = 8
    token = iota((ROWS, block_len), 1)

    def some_blocks(i, carry):
        scored = []
        for j in range(batch):
            b = i * batch + j
            s = lax.dot_general(
                q_recv[dest[b, 0]], kp[b], (((1,), (1,)), ((), ())), preferred_element_type=F32
            )
            scored.append(jnp.where(token < fill[b], s * scale, masked_score))
        s = jnp.concatenate(scored, axis=0)
        peak = jnp.max(s, axis=1, keepdims=True)
        w = jnp.exp(s - peak)
        total = jnp.sum(w, axis=1, keepdims=True)
        w16 = w.astype(BF16)
        mixed = jnp.concatenate(
            [
                jnp.dot(w16[j * ROWS : (j + 1) * ROWS], vp[i * batch + j], preferred_element_type=F32)
                for j in range(batch)
            ],
            axis=0,
        )
        first = pl.multiple_of(i * batch, batch)
        part[pl.ds(first, batch)] = (mixed / total).astype(BF16).reshape(batch, ROWS, HD)
        lse_blk[pl.ds(first, batch), :] = diagonal(peak + jnp.log(total))
        return carry

    lax.fori_loop(0, pool // batch, some_blocks, 0)

    def to_lane(l, carry):
        b = lane_blk[0, l]
        p_send[l] = part[b]
        l_send[pl.ds(l, 1), :] = lse_blk[pl.ds(b, 1), :]
        return carry

    lax.fori_loop(0, peers, to_lane, 0, unroll=8)
    p_recv[me] = p_send[me]
    l_recv[pl.ds(me, 1), :] = l_send[pl.ds(me, 1), :]
    to_roll(lambda d: p_send.at[d], p_recv.at[me], 2)
    to_roll(lambda d: l_send.at[pl.ds(d, 1), :], l_recv.at[pl.ds(me, 1), :], 3)

    wait_lanes(l_recv, recv_sem.at[3])
    tags = tagc[...]
    lse = jnp.where(tags >= 0.0, l_recv[...], masked_score)
    for s in range(slots):
        mine_s = jnp.where(tags == float(s), lse, masked_score)
        top_s[pl.ds(s, 1), :] = jnp.max(mine_s, axis=0, keepdims=True)
    top = jnp.maximum(top_s[...], new_peak)
    top_s[...] = top
    lane_top = jnp.zeros((peers, HD), F32)
    for s in range(slots):
        lane_top = jnp.where(tags == float(s), top_s[pl.ds(s, 1), :], lane_top)
    weight = jnp.exp(lse - lane_top)
    for s in range(slots):
        mine_s = jnp.where(tags == float(s), weight, 0.0)
        den_s[pl.ds(s, 1), :] = jnp.sum(mine_s, axis=0, keepdims=True)
    new_weight = jnp.exp(new_peak - top)
    inverse = 1.0 / (den_s[...] + new_total * new_weight)
    den_s[...] = inverse
    lane_inv = jnp.zeros((peers, HD), F32)
    for s in range(slots):
        lane_inv = jnp.where(tags == float(s), den_s[pl.ds(s, 1), :], lane_inv)
    wide[...] = weight * lane_inv
    new_share = new_weight * inverse

    wait_lanes(p_recv, recv_sem.at[2])
    on_row = iota((ROWS, HD), 0) == iota((ROWS, HD), 1)

    def weigh(l, carry):
        row = jnp.where(on_row, wide[pl.ds(l, 1), :], 0.0)
        column = jnp.sum(row, axis=1, keepdims=True)
        at = pl.ds(pl.multiple_of(l * ROWS, ROWS), ROWS)
        weighted[at, :] = (p_recv[l].astype(F32) * column).astype(BF16)
        return carry

    lax.fori_loop(0, peers, weigh, 0, unroll=8)
    mixed = jnp.dot(sel_t[...], weighted[...], preferred_element_type=F32)
    for r in range(rows):
        t, g = r // group, r % group
        at = slice(r * slots, (r + 1) * slots)
        res = mixed[at] + new_share[:, r : r + 1] * new_mixed[at, :]
        out_ref[t, :, g * HD : (g + 1) * HD] = res.astype(BF16)

    wait_learn(lq_recv, low_send_sem.at[0])
    wait_learn(lv_recv, low_send_sem.at[1])
    wait_lanes(tag_recv, send_sem.at[0])
    wait_lanes(q_recv, send_sem.at[1])
    wait_lanes(p_recv, send_sem.at[2])
    wait_lanes(l_recv, send_sem.at[3])


def on_device(
    x_rows,
    query_base_rows,
    k_base,
    value_base_rows,
    k_pool,
    v_pool,
    block_dest,
    block_slot,
    block_fill,
    a_query,
    query_up_factor,
    a_value,
    value_up_factor,
):
    peers, ranks = lax.axis_size("roll"), lax.axis_size("learn")
    steps, slots, width = x_rows.shape
    pool, block_len, _ = k_pool.shape
    rank = a_query.shape[1]
    group = query_base_rows.shape[2] // HD
    chunk = width // ranks
    half = steps * slots // 2
    dims = (steps, slots, chunk, pool, block_len, group)
    hbm = pl.BlockSpec(memory_space=pltpu.HBM)
    smem = pl.BlockSpec(memory_space=pltpu.SMEM)
    vmem = pltpu.VMEM
    dma = pltpu.SemaphoreType.DMA
    return pl.pallas_call(
        functools.partial(kernel, peers, ranks, dims),
        out_shape=jax.ShapeDtypeStruct(query_base_rows.shape, BF16),
        in_specs=[hbm] * 6 + [smem] * 3 + [hbm] * 4,
        out_specs=pl.BlockSpec(memory_space=pltpu.VMEM),
        scratch_shapes=[
            vmem((steps, slots, chunk), BF16),
            vmem(query_base_rows.shape, BF16),
            vmem(k_base.shape, BF16),
            vmem(value_base_rows.shape, BF16),
            vmem(k_pool.shape, BF16),
            vmem(v_pool.shape, BF16),
            vmem(a_query.shape, BF16),
            vmem(query_up_factor.shape, BF16),
            vmem(a_value.shape, BF16),
            vmem(value_up_factor.shape, BF16),
            vmem((1, HD), F32),
            vmem((peers, HD), F32),
            vmem((1, HD), jnp.int32),
            pltpu.SMEM((1, HD), jnp.int32),
            vmem((ranks, half, 2 * rank), F32),
            vmem((ranks, half, 2 * rank), F32),
            vmem((peers, HD), F32),
            vmem((peers * ROWS, ROWS * slots), BF16),
            vmem((ROWS * slots, peers * ROWS), BF16),
            vmem((peers, ROWS, HD), BF16),
            vmem((peers, ROWS, HD), BF16),
            vmem((pool, ROWS, HD), BF16),
            vmem((pool, HD), F32),
            vmem((peers, ROWS, HD), BF16),
            vmem((peers, ROWS, HD), BF16),
            vmem((peers, HD), F32),
            vmem((peers, HD), F32),
            vmem((ROWS * slots, HD), F32),
            vmem((slots, HD), F32),
            vmem((slots, HD), F32),
            vmem((peers, HD), F32),
            vmem((peers * ROWS, HD), BF16),
            dma((10,)),
            dma,
            dma((4,)),
            dma((4,)),
            dma((2,)),
            dma((2,)),
        ],
        compiler_params=pltpu.CompilerParams(
            collective_id=0, has_side_effects=True, vmem_limit_bytes=48 * 1024 * 1024
        ),
    )(
        x_rows,
        query_base_rows,
        k_base,
        value_base_rows,
        k_pool,
        v_pool,
        block_dest,
        block_slot,
        block_fill,
        a_query,
        query_up_factor,
        a_value,
        value_up_factor,
    )


def solution(mesh):
    return jax.shard_map(
        on_device,
        mesh=mesh,
        in_specs=(
            P(None, "roll", None),
            P(None, "roll", "learn"),
            P(None, "roll", "learn"),
            P(None, "roll", "learn"),
            P("roll", None, "learn"),
            P("roll", None, "learn"),
            P("roll", None),
            P("roll"),
            P("roll"),
            P("learn", None),
            P(None, "learn"),
            P("learn", None),
            P(None, "learn"),
        ),
        out_specs=P(None, "roll", "learn"),
        check_vma=False,
    )
```

time: 202 us -> 60.4 us (0.30)
  the two profiles are of different devices: /device:TPU:65 before, /device:TPU:64 now
where the time goes in v1:
time: 60.4 us; the launch traced here: 59.9 us
  Pallas kernels  49.5 us (82%)
  local copies, waits for them, and re-layouts  10.4 us (17%)
    pallas_call x1, Pallas kernels, on_device(): pl.pallas_call(functools.partial(kernel, peers, ranks, dims), out_shape=j...  49.5 us
    unnamed x24, local copies, waits for them, and re-layouts  10.4 us

profile of v1, /device:TPU:64, one launch (start us, length us, event | category | flops | bytes accessed | tf_op | source)
XLA Modules:
  0.0 59.9 jit_solution(8795588914980644177)
XLA Ops:
  0.0 0.0 copy-start.2
  0.0 0.8 %copy.14.dest = s32[32,1]{1,0:T(8,128)S(1)} copy(s32[32,1]{0,1:T(1,128)} %param.19) | data formatting | bytes 256 | tf_op args[6]
  0.8 1.0 %copy.15.aq_hbm = bf16[640,64]{1,0:T(8,128)(2,1)S(1)} copy(bf16[640,64]{0,1:T(8,128)(2,1)} %param.22) | data formatting | bytes 163840 | tf_op args[9]
  1.8 0.0 copy-start.5
  1.9 1.1 %copy.16.av_hbm = bf16[640,64]{1,0:T(8,128)(2,1)S(1)} copy(bf16[640,64]{0,1:T(8,128)(2,1)} %param.24) | data formatting | bytes 163840 | tf_op args[11]
  2.9 0.0 copy-done.2
  2.9 0.0 copy-done.5
  2.9 0.0 copy-start
  2.9 1.2 %copy-done = bf16[32,128,128]{2,1,0:T(8,128)(2,1)S(1)} copy-done((bf16[32,128,128]{2,1,0:T(8,128)(2,1)S(1)}, bf16[32,128,128]{2,1,0:T(8,128)(2,1)}, u32[]{:S(2)}) %copy-start) | copy-done | bytes 1048600
  4.2 0.0 copy-start.1
  4.2 1.2 %copy-done.1 = bf16[32,128,128]{2,1,0:T(8,128)(2,1)S(1)} copy-done((bf16[32,128,128]{2,1,0:T(8,128)(2,1)S(1)}, bf16[32,128,128]{2,1,0:T(8,128)(2,1)}, u32[]{:S(2)}) %copy-start.1) | copy-done | bytes 1048600
  5.4 0.0 copy-start.3
  5.4 0.9 %copy-done.3 = bf16[64,640]{1,0:T(8,128)(2,1)S(1)} copy-done((bf16[64,640]{1,0:T(8,128)(2,1)S(1)}, bf16[64,640]{1,0:T(8,128)(2,1)}, u32[]{:S(2)}) %copy-start.3) | copy-done | bytes 81944
  6.3 0.0 copy-start.4
  6.3 0.8 %copy-done.4 = bf16[3,16,640]{2,1,0:T(8,128)(2,1)S(1)} copy-done((bf16[3,16,640]{2,1,0:T(8,128)(2,1)S(1)}, bf16[3,16,640]{2,1,0:T(8,128)(2,1)}, u32[]{:S(2)}) %copy-start.4) | copy-done | bytes 61464
  7.1 0.0 copy-start.6
  7.1 0.7 %copy-done.6 = bf16[3,16,128]{2,1,0:T(8,128)(2,1)S(1)} copy-done((bf16[3,16,128]{2,1,0:T(8,128)(2,1)S(1)}, bf16[3,16,128]{2,1,0:T(8,128)(2,1)}, u32[]{:S(2)}) %copy-start.6) | copy-done | bytes 12312
  7.8 0.0 copy-start.7
  7.8 0.7 %copy-done.7 = bf16[3,16,128]{2,1,0:T(8,128)(2,1)S(1)} copy-done((bf16[3,16,128]{2,1,0:T(8,128)(2,1)S(1)}, bf16[3,16,128]{2,1,0:T(8,128)(2,1)}, u32[]{:S(2)}) %copy-start.7) | copy-done | bytes 12312
  8.5 0.0 copy-start.8
  8.5 0.7 %copy-done.8 = s32[32]{0:T(128)S(1)} copy-done((s32[32]{0:T(128)S(1)}, s32[32]{0:T(128)}, u32[]{:S(2)}) %copy-start.8) | copy-done | bytes 152
  9.2 0.0 copy-start.9
  9.2 0.7 %copy-done.9 = s32[32]{0:T(128)S(1)} copy-done((s32[32]{0:T(128)S(1)}, s32[32]{0:T(128)}, u32[]{:S(2)}) %copy-start.9) | copy-done | bytes 152
  9.8 49.5 %shard_map.127 = bf16[3,16,640]{2,1,0:T(8,128)(2,1)S(1)} custom-call(bf16[3,16,5120]{2,1,0:T(8,128)(2,1)S(1)} %copy-done.2, bf16[3,16,640]{2,1,0:T(8,128)(2,1)S(1)} %copy-done.4, bf16[3,16,128]{2,1,0:T(8,128)(2,1)S(1)} %copy-done.6, bf16[3,16,128]{2,1,0:T(8,128)(2,1)S(1)} %copy-done.7, bf16[32,128,128]{2,1,0:T(8,128)(2,1)S(1)} %copy-done, ...), custom_call_target="tpu_custom_call" | custom-call | tf_op jit(solution)/shard_map/pallas_call | solution.py:388
  59.3 0.6 %copy.18 = bf16[3,16,640]{2,1,0:T(8,128)(2,1)} copy(bf16[3,16,640]{2,1,0:T(8,128)(2,1)S(1)} %shard_map.127) | data formatting | bytes 122880
Async XLA Ops:
  0.0 2.9 %copy-start.2 = (bf16[3,16,5120]{2,1,0:T(8,128)(2,1)S(1)}, bf16[3,16,5120]{2,1,0:T(8,128)(2,1)}, u32[]{:S(2)}) copy-start(bf16[3,16,5120]{2,1,0:T(8,128)(2,1)} %x_hbm.1) | copy-start | bytes 1474564
  1.8 1.1 %copy-start.5 = (bf16[64,128]{1,0:T(8,128)(2,1)S(1)}, bf16[64,128]{1,0:T(8,128)(2,1)}, u32[]{:S(2)}) copy-start(bf16[64,128]{1,0:T(8,128)(2,1)} %vu_hbm.1) | copy-start | bytes 49156
  2.9 1.2 %copy-start = (bf16[32,128,128]{2,1,0:T(8,128)(2,1)S(1)}, bf16[32,128,128]{2,1,0:T(8,128)(2,1)}, u32[]{:S(2)}) copy-start(bf16[32,128,128]{2,1,0:T(8,128)(2,1)} %kp_hbm.1) | copy-start | bytes 3145732
  4.2 1.2 %copy-start.1 = (bf16[32,128,128]{2,1,0:T(8,128)(2,1)S(1)}, bf16[32,128,128]{2,1,0:T(8,128)(2,1)}, u32[]{:S(2)}) copy-start(bf16[32,128,128]{2,1,0:T(8,128)(2,1)} %vp_hbm.1) | copy-start | bytes 3145732
  5.4 0.9 %copy-start.3 = (bf16[64,640]{1,0:T(8,128)(2,1)S(1)}, bf16[64,640]{1,0:T(8,128)(2,1)}, u32[]{:S(2)}) copy-start(bf16[64,640]{1,0:T(8,128)(2,1)} %qu_hbm.1) | copy-start | bytes 245764
  6.3 0.8 %copy-start.4 = (bf16[3,16,640]{2,1,0:T(8,128)(2,1)S(1)}, bf16[3,16,640]{2,1,0:T(8,128)(2,1)}, u32[]{:S(2)}) copy-start(bf16[3,16,640]{2,1,0:T(8,128)(2,1)} %qb_hbm.1) | copy-start | bytes 184324
  7.1 0.7 %copy-start.6 = (bf16[3,16,128]{2,1,0:T(8,128)(2,1)S(1)}, bf16[3,16,128]{2,1,0:T(8,128)(2,1)}, u32[]{:S(2)}) copy-start(bf16[3,16,128]{2,1,0:T(8,128)(2,1)} %kb_hbm.1) | copy-start | bytes 36868
  7.8 0.7 %copy-start.7 = (bf16[3,16,128]{2,1,0:T(8,128)(2,1)S(1)}, bf16[3,16,128]{2,1,0:T(8,128)(2,1)}, u32[]{:S(2)}) copy-start(bf16[3,16,128]{2,1,0:T(8,128)(2,1)} %vb_hbm.1) | copy-start | bytes 36868
  8.5 0.7 %copy-start.8 = (s32[32]{0:T(128)S(1)}, s32[32]{0:T(128)}, u32[]{:S(2)}) copy-start(s32[32]{0:T(128)} %slot.1) | copy-start | bytes 388
  9.2 0.7 %copy-start.9 = (s32[32]{0:T(128)S(1)}, s32[32]{0:T(128)}, u32[]{:S(2)}) copy-start(s32[32]{0:T(128)} %fill.1) | copy-start | bytes 388

commit v2 on v1

--- a/solution.py
+++ b/solution.py
@@ -22,11 +22,18 @@
     return lax.broadcasted_iota(jnp.int32, shape, dim)
 
 
-def diagonal(column):
+def in_spare_row(column, tiles):
     n = column.shape[0]
-    here = iota((n, HD), 1) == lax.rem(iota((n, HD), 0), ROWS)
-    spread = jnp.where(here, jnp.broadcast_to(column, (n, HD)), 0.0)
-    return jnp.sum(spread.reshape(n // ROWS, ROWS, HD), axis=1)
+    row, lane = lax.rem(iota((n, HD), 0), ROWS), iota((n, HD), 1)
+    high = column.astype(BF16).astype(F32)
+    middle = (column - high).astype(BF16).astype(F32)
+    low = column - high - middle
+    spread = jnp.where(lane == row, high, 0.0)
+    spread = jnp.where(lane == row + ROWS, middle, spread)
+    spread = jnp.where(lane == row + 2 * ROWS, low, spread)
+    line = jnp.sum(spread.reshape(n // ROWS, ROWS, HD), axis=1, keepdims=True)
+    tiles = tiles.reshape(n // ROWS, ROWS, HD)
+    return jnp.where(iota(tiles.shape, 1) == ROWS - 1, line, tiles)
 
 
 def kernel(
@@ -53,27 +60,23 @@
     vb,
     kp,
     vp,
-    aq,
+    a_both,
     qu,
-    av,
     vu,
     tag_send,
     tag_recv,
     lane_vec,
     lane_blk,
-    lq_recv,
-    lv_recv,
+    low_recv,
+    low_total,
     tagc,
     sel,
     sel_t,
     q_send,
     q_recv,
     part,
-    lse_blk,
     p_send,
     p_recv,
-    l_send,
-    l_recv,
     new_mixed,
     top_s,
     den_s,
@@ -85,31 +88,30 @@
     recv_sem,
     low_send_sem,
     low_recv_sem,
+    inner_in,
+    roll_in,
 ):
     steps, slots, chunk, pool, block_len, group = dims
     rows = steps * group
+    rank = aq_hbm.shape[0]
     me, ml = lax.axis_index("roll"), lax.axis_index("learn")
     others = pl.ds(0, peers - 1)
 
+    chips = ranks // 2
+    chip, core = ml // 2, lax.rem(ml, 2)
+    partner = ml + 1 - 2 * core
+    is_inner, is_outer = chip < 2, chip >= 2
+    is_outer0 = jnp.logical_and(is_outer, core == 0)
+    is_outer1 = jnp.logical_and(is_outer, core == 1)
+    n_inner = 4
     barrier = pltpu.get_barrier_semaphore()
-
-    def greet(i, carry):
-        pl.semaphore_signal(
-            barrier, inc=1, device_id=(lax.rem(me + i, peers), ml), device_id_type=MESH
-        )
-        return carry
-
-    lax.fori_loop(1, peers, greet, 0)
-    for i in range(1, ranks):
-        pl.semaphore_signal(
-            barrier, inc=1, device_id=(me, lax.rem(ml + i, ranks)), device_id_type=MESH
-        )
+    gatherer = ml - core * (chip // 2)
 
     start = pl.multiple_of(ml * chunk, HD)
     pairs = [
         (x_hbm.at[:, :, pl.ds(start, chunk)], x),
-        (aq_hbm, aq),
-        (av_hbm, av),
+        (aq_hbm, a_both.at[pl.ds(0, rank)]),
+        (av_hbm, a_both.at[pl.ds(rank, rank)]),
         (qb_hbm, qb),
         (qu_hbm, qu),
         (kb_hbm, kb),
@@ -119,14 +121,87 @@
         (vp_hbm, vp),
     ]
     loads = [pltpu.make_async_copy(a, b, local_sem.at[i]) for i, (a, b) in enumerate(pairs)]
-    for load in loads:
+    for load in loads[:3]:
         load.start()
+
+    def signal(sem, roll, learn):
+        pl.semaphore_signal(sem, inc=1, device_id=(roll, learn), device_id_type=MESH)
+
+    def greet(i, carry):
+        signal(barrier, lax.rem(me + i, peers), gatherer)
+        return carry
+
+    signal(barrier, me, partner)
+
+    @pl.when(is_inner)
+    def _():
+        signal(barrier, me, 2 - 2 * chip)
+        signal(barrier, me, 3 - 2 * chip)
+        for j in range(2, chips):
+            signal(barrier, me, 2 * j + 1)
+
+    @pl.when(is_inner)
+    def _():
+        lax.fori_loop(1, peers, greet, 0, unroll=7)
+
+    for load in loads[3:]:
+        load.start()
+
+    for load in loads[:3]:
+        load.wait()
+    partial = lax.dot_general(
+        x[...].reshape(steps * slots, chunk),
+        a_both[...],
+        (((1,), (1,)), ((), ())),
+        preferred_element_type=F32,
+    )
+    low_recv[ml] = partial.astype(BF16)
+
+    def to_learn(src, dst, k, learn):
+        return pltpu.make_async_remote_copy(
+            src_ref=src,
+            dst_ref=dst,
+            send_sem=low_send_sem.at[k],
+            recv_sem=low_recv_sem.at[k],
+            device_id=(me, learn),
+            device_id_type=MESH,
+        )
+
+    @pl.when(is_inner)
+    def _():
+        pl.semaphore_wait(barrier, peers + 2)
+
+    @pl.when(is_outer1)
+    def _():
+        pl.semaphore_wait(barrier, n_inner + 1)
+        signal(inner_in, me, partner)
+
+    @pl.when(is_outer0)
+    def _():
+        pl.semaphore_wait(inner_in, 1)
+
+    mine = low_recv.at[ml]
+
+    @pl.when(is_inner)
+    def _():
+        to_learn(mine, mine, 0, partner).start()
+        to_learn(mine, mine, 0, 2 - 2 * chip).start()
+        to_learn(mine, mine, 0, 3 - 2 * chip).start()
+
+    @pl.when(is_outer)
+    def _():
+        for j in range(n_inner):
+            to_learn(mine, mine, 0, j).start()
+
+    @pl.when(is_outer)
+    def _():
+        lax.fori_loop(1, peers, greet, 0, unroll=7)
 
     lane = iota((1, HD), 1)
     tag_row = jnp.full((1, HD), no_slot, F32)
     blk_row = jnp.zeros((1, HD), jnp.int32)
     for b in range(pool):
-        hit = lane == dest[b, 0]
+        hit = lane == dest[0, b]
         tag_row = jnp.where(hit, slot[b].astype(F32), tag_row)
         blk_row = jnp.where(hit, b, blk_row)
     tag_send[...] = tag_row
@@ -135,36 +210,14 @@
     to_smem = pltpu.make_async_copy(lane_vec, lane_blk, blk_sem)
     to_smem.start()
 
-    for load in loads[:3]:
-        load.wait()
-    x_rows = x[...].reshape(steps * slots, chunk)
-    half = steps * slots // 2
-
-    def packed(a):
-        low = jnp.dot(x_rows, a[...], preferred_element_type=F32)
-        return jnp.concatenate([low[:half], low[half:]], axis=1)
-
-    lq_recv[ml] = packed(aq)
-    lv_recv[ml] = packed(av)
-
-    pl.semaphore_wait(barrier, peers + ranks - 2)
-
-    def to_learn(buf, k):
-        copies = []
-        for i in range(1, ranks):
-            copies.append(
-                pltpu.make_async_remote_copy(
-                    src_ref=buf.at[ml],
-                    dst_ref=buf.at[ml],
-                    send_sem=low_send_sem.at[k],
-                    recv_sem=low_recv_sem.at[k],
-                    device_id=(me, lax.rem(ml + i, ranks)),
-                    device_id_type=MESH,
-                )
-            )
-            copies[-1].start()
-
-    to_learn(lq_recv, 0)
+    @pl.when(is_outer0)
+    def _():
+        pl.semaphore_wait(barrier, 2 * peers - 1)
+        signal(roll_in, me, partner)
+
+    @pl.when(is_outer1)
+    def _():
+        pl.semaphore_wait(roll_in, 1)
 
     def to_roll(src_of, dst, k):
         def one(i, carry):
@@ -182,14 +235,13 @@
         lax.fori_loop(1, peers, one, 0)
 
     to_roll(lambda d: tag_send, tag_recv.at[pl.ds(me, 1), :], 0)
-    to_learn(lv_recv, 1)
+
 
     def wait_lanes(buf, sem):
         pltpu.make_async_copy(buf.at[others], buf.at[others], sem).wait()
 
-    def wait_learn(buf, sem):
-        rest = buf.at[pl.ds(0, ranks - 1)]
-        pltpu.make_async_copy(rest, rest, sem).wait()
+    def wait_for(ref, sem):
+        pltpu.make_async_copy(ref, ref, sem).wait()
 
     wait_lanes(tag_recv, recv_sem.at[0])
     mine = iota((peers, HD), 1) == me
@@ -209,17 +261,21 @@
 
     lax.fori_loop(0, peers, pick, 0, unroll=8)
 
-    def unpacked(buf):
-        low = buf[0]
-        for i in range(1, ranks):
-            low = low + buf[i]
-        rank = low.shape[1] // 2
-        return jnp.concatenate([low[:, :rank], low[:, rank:]], axis=0).astype(BF16)
-
     for load in loads[3:5]:
         load.wait()
-    wait_learn(lq_recv, low_recv_sem.at[0])
-    up = jnp.dot(unpacked(lq_recv), qu[...], preferred_element_type=F32)
+
+    @pl.when(is_inner)
+    def _():
+        wait_for(low_recv.at[pl.ds(0, ranks - 1)], low_recv_sem.at[0])
+        summed = functools.reduce(jnp.add, [low_recv[j].astype(F32) for j in range(ranks)])
+        low_total[...] = summed.astype(BF16)
+        to_learn(low_total, low_total, 1, 2 * (chips - 1 - chip) + core).start()
+
+    @pl.when(is_outer)
+    def _():
+        wait_for(low_total, low_recv_sem.at[1])
+
+    up = jnp.dot(low_total[:, :rank], qu[...], preferred_element_type=F32)
     query = qb[...].reshape(steps * slots, group * HD).astype(F32) + adapter_scale * up
     query = query.astype(BF16)
     tiles = [
@@ -234,15 +290,57 @@
     to_roll(lambda d: q_send.at[d], q_recv.at[me], 1)
 
     sel_t[...] = sel[...].T
+
+    for load in loads[8:]:
+        load.wait()
+    to_smem.wait()
+    wait_lanes(q_recv, recv_sem.at[1])
+    scale = 1.0 / math.sqrt(HD)
+    batch = 8
+    token = iota((ROWS, block_len), 1)
+
+    def some_blocks(i, carry):
+        scored = []
+        for j in range(batch):
+            b = i * batch + j
+            s = lax.dot_general(
+                q_recv[dest[0, b]], kp[b], (((1,), (1,)), ((), ())), preferred_element_type=F32
+            )
+            scored.append(jnp.where(token < fill[b], s * scale, masked_score))
+        s = jnp.concatenate(scored, axis=0)
+        peak = jnp.max(s, axis=1, keepdims=True)
+        w = jnp.exp(s - peak)
+        total = jnp.sum(w, axis=1, keepdims=True)
+        w16 = w.astype(BF16)
+        mixed = jnp.concatenate(
+            [
+                jnp.dot(w16[j * ROWS : (j + 1) * ROWS], vp[i * batch + j], preferred_element_type=F32)
+                for j in range(batch)
+            ],
+            axis=0,
+        )
+        first = pl.multiple_of(i * batch, batch)
+        tiles = in_spare_row(peak + jnp.log(total), mixed / total)
+        part[pl.ds(first, batch)] = tiles.astype(BF16)
+        return carry
+
+    lax.fori_loop(0, pool // batch, some_blocks, 0)
+
+    def to_lane(l, carry):
+        p_send[l] = part[lane_blk[0, l]]
+        return carry
+
+    lax.fori_loop(0, peers, to_lane, 0, unroll=8)
+    p_recv[me] = p_send[me]
+    to_roll(lambda d: p_send.at[d], p_recv.at[me], 2)
+
     for load in loads[5:8]:
         load.wait()
-    wait_learn(lv_recv, low_recv_sem.at[1])
-    up_v = jnp.dot(unpacked(lv_recv), vu[...], preferred_element_type=F32)
+    up_v = jnp.dot(low_total[:, rank:], vu[...], preferred_element_type=F32)
     value = vb[...].reshape(steps * slots, HD).astype(F32) + adapter_scale * up_v
     value = value.astype(BF16).astype(F32)
     values = [value[t * slots : (t + 1) * slots] for t in range(steps)]
     keys = [kb[t].astype(F32) for t in range(steps)]
-    scale = 1.0 / math.sqrt(HD)
     lane_s = iota((slots, HD), 1)
     scores = [jnp.full((slots, HD), masked_score, F32) for _ in range(steps)]
     for r in range(rows):
@@ -262,55 +360,17 @@
             acc = acc + rounded[u][:, r : r + 1] * values[u]
         new_mixed[pl.ds(r * slots, slots), :] = acc
 
-    for load in loads[8:]:
-        load.wait()
-    to_smem.wait()
-    wait_lanes(q_recv, recv_sem.at[1])
-    batch = 8
-    token = iota((ROWS, block_len), 1)
-
-    def some_blocks(i, carry):
-        scored = []
-        for j in range(batch):
-            b = i * batch + j
-            s = lax.dot_general(
-                q_recv[dest[b, 0]], kp[b], (((1,), (1,)), ((), ())), preferred_element_type=F32
-            )
-            scored.append(jnp.where(token < fill[b], s * scale, masked_score))
-        s = jnp.concatenate(scored, axis=0)
-        peak = jnp.max(s, axis=1, keepdims=True)
-        w = jnp.exp(s - peak)
-        total = jnp.sum(w, axis=1, keepdims=True)
-        w16 = w.astype(BF16)
-        mixed = jnp.concatenate(
-            [
-                jnp.dot(w16[j * ROWS : (j + 1) * ROWS], vp[i * batch + j], preferred_element_type=F32)
-                for j in range(batch)
-            ],
-            axis=0,
-        )
-        first = pl.multiple_of(i * batch, batch)
-        part[pl.ds(first, batch)] = (mixed / total).astype(BF16).reshape(batch, ROWS, HD)
-        lse_blk[pl.ds(first, batch), :] = diagonal(peak + jnp.log(total))
+    wait_lanes(p_recv, recv_sem.at[2])
+
+    def spare_row(l, carry):
+        wide[pl.ds(l, 1), :] = p_recv[l].astype(F32)[ROWS - 1 :]
         return carry
 
-    lax.fori_loop(0, pool // batch, some_blocks, 0)
-
-    def to_lane(l, carry):
-        b = lane_blk[0, l]
-        p_send[l] = part[b]
-        l_send[pl.ds(l, 1), :] = lse_blk[pl.ds(b, 1), :]
-        return carry
-
-    lax.fori_loop(0, peers, to_lane, 0, unroll=8)
-    p_recv[me] = p_send[me]
-    l_recv[pl.ds(me, 1), :] = l_send[pl.ds(me, 1), :]
-    to_roll(lambda d: p_send.at[d], p_recv.at[me], 2)
-    to_roll(lambda d: l_send.at[pl.ds(d, 1), :], l_recv.at[pl.ds(me, 1), :], 3)
-
-    wait_lanes(l_recv, recv_sem.at[3])
+    lax.fori_loop(0, peers, spare_row, 0, unroll=8)
     tags = tagc[...]
-    lse = jnp.where(tags >= 0.0, l_recv[...], masked_score)
+    line = wide[...]
+    middle, low = pltpu.roll(line, HD - ROWS, 1), pltpu.roll(line, HD - 2 * ROWS, 1)
+    lse = jnp.where(tags >= 0.0, line + middle + low, masked_score)
     for s in range(slots):
         mine_s = jnp.where(tags == float(s), lse, masked_score)
         top_s[pl.ds(s, 1), :] = jnp.max(mine_s, axis=0, keepdims=True)
@@ -332,7 +392,6 @@
     wide[...] = weight * lane_inv
     new_share = new_weight * inverse
 
-    wait_lanes(p_recv, recv_sem.at[2])
     on_row = iota((ROWS, HD), 0) == iota((ROWS, HD), 1)
 
     def weigh(l, carry):
@@ -350,12 +409,18 @@
         res = mixed[at] + new_share[:, r : r + 1] * new_mixed[at, :]
         out_ref[t, :, g * HD : (g + 1) * HD] = res.astype(BF16)
 
-    wait_learn(lq_recv, low_send_sem.at[0])
-    wait_learn(lv_recv, low_send_sem.at[1])
+    @pl.when(is_inner)
+    def _():
+        wait_for(low_recv.at[pl.ds(0, n_inner - 1)], low_send_sem.at[0])
+        wait_for(low_total, low_send_sem.at[1])
+
+    @pl.when(is_outer)
+    def _():
+        wait_for(low_recv.at[pl.ds(0, n_inner)], low_send_sem.at[0])
+
     wait_lanes(tag_recv, send_sem.at[0])
     wait_lanes(q_recv, send_sem.at[1])
     wait_lanes(p_recv, send_sem.at[2])
-    wait_lanes(l_recv, send_sem.at[3])
 
 
 def on_device(
@@ -377,9 +442,9 @@
     steps, slots, width = x_rows.shape
     pool, block_len, _ = k_pool.shape
     rank = a_query.shape[1]
+    a_query, a_value, block_dest = a_query.T, a_value.T, block_dest.T
     group = query_base_rows.shape[2] // HD
     chunk = width // ranks
-    half = steps * slots // 2
     dims = (steps, slots, chunk, pool, block_len, group)
     hbm = pl.BlockSpec(memory_space=pltpu.HBM)
     smem = pl.BlockSpec(memory_space=pltpu.SMEM)
@@ -397,27 +462,23 @@
             vmem(value_base_rows.shape, BF16),
             vmem(k_pool.shape, BF16),
             vmem(v_pool.shape, BF16),
-            vmem(a_query.shape, BF16),
+            vmem((2 * rank, chunk), BF16),
             vmem(query_up_factor.shape, BF16),
-            vmem(a_value.shape, BF16),
             vmem(value_up_factor.shape, BF16),
             vmem((1, HD), F32),
             vmem((peers, HD), F32),
             vmem((1, HD), jnp.int32),
             pltpu.SMEM((1, HD), jnp.int32),
-            vmem((ranks, half, 2 * rank), F32),
-            vmem((ranks, half, 2 * rank), F32),
+            vmem((ranks, steps * slots, 2 * rank), BF16),
+            vmem((steps * slots, 2 * rank), BF16),
             vmem((peers, HD), F32),
             vmem((peers * ROWS, ROWS * slots), BF16),
             vmem((ROWS * slots, peers * ROWS), BF16),
             vmem((peers, ROWS, HD), BF16),
             vmem((peers, ROWS, HD), BF16),
             vmem((pool, ROWS, HD), BF16),
-            vmem((pool, HD), F32),
             vmem((peers, ROWS, HD), BF16),
             vmem((peers, ROWS, HD), BF16),
-            vmem((peers, HD), F32),
-            vmem((peers, HD), F32),
             vmem((ROWS * slots, HD), F32),
             vmem((slots, HD), F32),
             vmem((slots, HD), F32),
@@ -425,13 +486,15 @@
             vmem((peers * ROWS, HD), BF16),
             dma((10,)),
             dma,
-            dma((4,)),
-            dma((4,)),
+            dma((3,)),
+            dma((3,)),
             dma((2,)),
             dma((2,)),
+            pltpu.SemaphoreType.REGULAR,
+            pltpu.SemaphoreType.REGULAR,
         ],
         compiler_params=pltpu.CompilerParams(
-            collective_id=0, has_side_effects=True, vmem_limit_bytes=48 * 1024 * 1024
+            collective_id=0, has_side_effects=True, vmem_limit_bytes=64 * 1024 * 1024
         ),
     )(
         x_rows,

time: 60.4 us -> 44.4 us (0.74)
  the two profiles are of different devices: /device:TPU:64 before, /device:TPU:24 now
where the time goes in v2:
time: 44.4 us; the launch traced here: 44.2 us
  Pallas kernels  42.7 us (96%)
  local copies, waits for them, and re-layouts  1.46 us (3%)
    pallas_call x1, Pallas kernels, on_device(): pl.pallas_call(functools.partial(kernel, peers, ranks, dims), out_shape=j...  42.7 us
    unnamed x1, local copies, waits for them, and re-layouts  1.46 us

profile of v2, /device:TPU:24, one launch (start us, length us, event | category | flops | bytes accessed | tf_op | source)
XLA Modules:
  0.0 44.2 jit_solution(16008024088954177987)
XLA Ops:
  0.0 42.7 %shard_map.127 = bf16[3,16,640]{2,1,0:T(8,128)(2,1)} custom-call(bf16[3,16,5120]{2,1,0:T(8,128)(2,1)} %x_hbm.1, bf16[3,16,640]{2,1,0:T(8,128)(2,1)} %qb_hbm.1, bf16[3,16,128]{2,1,0:T(8,128)(2,1)} %kb_hbm.1, bf16[3,16,128]{2,1,0:T(8,128)(2,1)} %vb_hbm.1, bf16[32,128,128]{2,1,0:T(8,128)(2,1)} %kp_hbm.1, bf16[32,128,128]{2,1,0:T(8,128)(2,1)} %vp_hbm.1, ...), custom_call_target="tpu_custom_call" | custom-call | tf_op jit(solution)/shard_map/pallas_call | solution.py:453
  42.7 1.5 %copy.15 = bf16[3,16,640]{2,1,0:T(8,128)(2,1)} copy(bf16[3,16,640]{2,1,0:T(8,128)(2,1)} %shard_map.127) | data formatting | bytes 122880

commit v3 on v2

--- a/solution.py
+++ b/solution.py
@@ -46,15 +46,18 @@
     vb_hbm,
     kp_hbm,
     vp_hbm,
-    dest,
-    slot,
-    fill,
+    dest_hbm,
+    slot_hbm,
+    fill_hbm,
     aq_hbm,
     qu_hbm,
     av_hbm,
     vu_hbm,
     out_ref,
     x,
+    dest,
+    slot,
+    fill,
     qb,
     kb,
     vb,
@@ -74,7 +77,6 @@
     sel_t,
     q_send,
     q_recv,
-    part,
     p_send,
     p_recv,
     new_mixed,
@@ -86,6 +88,7 @@
     blk_sem,
     send_sem,
     recv_sem,
+    group_sem,
     low_send_sem,
     low_recv_sem,
     inner_in,
@@ -119,6 +122,9 @@
         (vu_hbm, vu),
         (kp_hbm, kp),
         (vp_hbm, vp),
+        (dest_hbm, dest),
+        (slot_hbm, slot),
+        (fill_hbm, fill),
     ]
     loads = [pltpu.make_async_copy(a, b, local_sem.at[i]) for i, (a, b) in enumerate(pairs)]
     for load in loads[:3]:
@@ -180,23 +186,25 @@
     def _():
         pl.semaphore_wait(inner_in, 1)
 
-    mine = low_recv.at[ml]
+    my_low = low_recv.at[ml]
 
     @pl.when(is_inner)
     def _():
-        to_learn(mine, mine, 0, partner).start()
-        to_learn(mine, mine, 0, 2 - 2 * chip).start()
-        to_learn(mine, mine, 0, 3 - 2 * chip).start()
+        to_learn(my_low, my_low, 0, partner).start()
+        to_learn(my_low, my_low, 0, 2 - 2 * chip).start()
+        to_learn(my_low, my_low, 0, 3 - 2 * chip).start()
 
     @pl.when(is_outer)
     def _():
         for j in range(n_inner):
-            to_learn(mine, mine, 0, j).start()
+            to_learn(my_low, my_low, 0, j).start()
 
     @pl.when(is_outer)
     def _():
         lax.fori_loop(1, peers, greet, 0, unroll=7)
 
+    for load in loads[10:12]:
+        load.wait()
     lane = iota((1, HD), 1)
     tag_row = jnp.full((1, HD), no_slot, F32)
     blk_row = jnp.zeros((1, HD), jnp.int32)
@@ -234,6 +242,49 @@
 
         lax.fori_loop(1, peers, one, 0)
 
+    side = 4
+    plane = side * side
+    my_y, my_z, my_x = me // plane, lax.rem(me // side, side), lax.rem(me, side)
+    z_of = [my_z, my_z + 1 - 2 * lax.rem(my_z, 2), lax.rem(my_z + 2, side), side - 1 - my_z]
+
+    def lane_at(c, i):
+        over = lax.rem(2 * (i // side), side) + i // (2 * side)
+        return (
+            lax.rem(my_y + over, side) * plane
+            + z_of[c] * side
+            + lax.rem(my_x + lax.rem(i, side), side)
+        )
+
+    batch = 8
+    groups = [(c, f) for c in range(side) for f in range(0, plane, batch)]
+
+    def lanes_of(group):
+        c, f = group
+        return [lane_at(c, f + j) for j in range(batch)]
+
+    def to_group(group, src, dst, k):
+        c, f = group
+        n = (c * plane + f) // batch
+
+        def one(j, carry):
+            d = lane_at(c, f + j)
+            pltpu.make_async_remote_copy(
+                src_ref=src.at[n * batch + j],
+                dst_ref=dst.at[me],
+                send_sem=send_sem.at[k],
+                recv_sem=group_sem.at[k - 1, n],
+                device_id=(d, ml),
+                device_id_type=MESH,
+            ).start()
+            return carry
+
+        lax.fori_loop(int(n == 0), batch, one, 0)
+
+    def wait_group(group, buf, k):
+        c, f = group
+        n = (c * plane + f) // batch
+        wait_for(buf.at[pl.ds(0, batch - int(n == 0))], group_sem.at[k - 1, n])
+
     to_roll(lambda d: tag_send, tag_recv.at[pl.ds(me, 1), :], 0)
 
 
@@ -252,14 +303,15 @@
     sel_row = (iota((ROWS, width), 0) * slots).astype(F32)
     sel_lane = iota((ROWS, width), 1).astype(F32)
 
-    def pick(l, carry):
-        row = tagc[pl.ds(l, 1), :]
+    def pick(c, i, carry):
+        row = tagc[pl.ds(lane_at(c, i), 1), :]
         want = sel_row + jnp.concatenate([row] * (width // HD), axis=1)
         hot = jnp.where(want == sel_lane, 1.0, 0.0).astype(BF16)
-        sel[pl.ds(pl.multiple_of(l * ROWS, ROWS), ROWS), :] = hot
+        sel[pl.ds(pl.multiple_of((c * plane + i) * ROWS, ROWS), ROWS), :] = hot
         return carry
 
-    lax.fori_loop(0, peers, pick, 0, unroll=8)
+    for c in range(side):
+        lax.fori_loop(0, plane, functools.partial(pick, c), 0, unroll=8)
 
     for load in loads[3:5]:
         load.wait()
@@ -284,55 +336,55 @@
         for g in range(group)
     ]
     stack = jnp.concatenate(tiles + [jnp.zeros((slots, HD), BF16)] * (ROWS - rows), axis=0)
-    picked = jnp.dot(sel[...], stack, preferred_element_type=F32).astype(BF16)
-    q_send[...] = picked.reshape(peers, ROWS, HD)
-    q_recv[me] = q_send[me]
-    to_roll(lambda d: q_send.at[d], q_recv.at[me], 1)
+    for c in range(side):
+        mine = pl.ds(c * plane * ROWS, plane * ROWS)
+        picked = jnp.dot(sel[mine, :], stack, preferred_element_type=F32).astype(BF16)
+        q_send[pl.ds(c * plane, plane)] = picked.reshape(plane, ROWS, HD)
+        for f in range(0, plane, batch):
+            to_group((c, f), q_send, q_recv, 1)
+    q_recv[me] = q_send[0]
 
     sel_t[...] = sel[...].T
 
-    for load in loads[8:]:
+    for load in loads[8:10] + loads[12:]:
         load.wait()
     to_smem.wait()
-    wait_lanes(q_recv, recv_sem.at[1])
     scale = 1.0 / math.sqrt(HD)
-    batch = 8
     token = iota((ROWS, block_len), 1)
 
-    def some_blocks(i, carry):
+    def some_lanes(group):
+        lanes = lanes_of(group)
+        first = group[0] * plane + group[1]
+        blocks = [lane_blk[0, d] for d in lanes]
         scored = []
-        for j in range(batch):
-            b = i * batch + j
+        for j in range(0, batch, 2):
+            queries = jnp.concatenate([q_recv[d] for d in lanes[j : j + 2]], axis=0)
+            keys = jnp.concatenate([kp[b] for b in blocks[j : j + 2]], axis=0)
             s = lax.dot_general(
-                q_recv[dest[0, b]], kp[b], (((1,), (1,)), ((), ())), preferred_element_type=F32
+                queries, keys, (((1,), (1,)), ((), ())), preferred_element_type=F32
             )
-            scored.append(jnp.where(token < fill[b], s * scale, masked_score))
+            for h in range(2):
+                own = s[h * ROWS : (h + 1) * ROWS, h * block_len : (h + 1) * block_len]
+                scored.append(jnp.where(token < fill[blocks[j + h]], own * scale, masked_score))
         s = jnp.concatenate(scored, axis=0)
         peak = jnp.max(s, axis=1, keepdims=True)
         w = jnp.exp(s - peak)
         total = jnp.sum(w, axis=1, keepdims=True)
         w16 = w.astype(BF16)
-        mixed = jnp.concatenate(
-            [
-                jnp.dot(w16[j * ROWS : (j + 1) * ROWS], vp[i * batch + j], preferred_element_type=F32)
-                for j in range(batch)
-            ],
-            axis=0,
-        )
-        first = pl.multiple_of(i * batch, batch)
-        tiles = in_spare_row(peak + jnp.log(total), mixed / total)
-        part[pl.ds(first, batch)] = tiles.astype(BF16)
-        return carry
-
-    lax.fori_loop(0, pool // batch, some_blocks, 0)
-
-    def to_lane(l, carry):
-        p_send[l] = part[lane_blk[0, l]]
-        return carry
-
-    lax.fori_loop(0, peers, to_lane, 0, unroll=8)
-    p_recv[me] = p_send[me]
-    to_roll(lambda d: p_send.at[d], p_recv.at[me], 2)
+        mixed = []
+        for j in range(0, batch, 2):
+            values = jnp.concatenate([vp[b] for b in blocks[j : j + 2]], axis=1)
+            m = jnp.dot(w16[j * ROWS : (j + 2) * ROWS], values, preferred_element_type=F32)
+            mixed += [m[:ROWS, :HD], m[ROWS:, HD:]]
+        mixed = jnp.concatenate(mixed, axis=0)
+        tiles = in_spare_row(peak + jnp.log(total), mixed / total).astype(BF16)
+        p_send[pl.ds(first, batch)] = tiles
+
+    for lanes_group in groups:
+        wait_group(lanes_group, q_recv, 1)
+        some_lanes(lanes_group)
+        to_group(lanes_group, p_send, p_recv, 2)
+    p_recv[me] = p_send[0]
 
     for load in loads[5:8]:
         load.wait()
@@ -360,13 +412,15 @@
             acc = acc + rounded[u][:, r : r + 1] * values[u]
         new_mixed[pl.ds(r * slots, slots), :] = acc
 
-    wait_lanes(p_recv, recv_sem.at[2])
-
-    def spare_row(l, carry):
-        wide[pl.ds(l, 1), :] = p_recv[l].astype(F32)[ROWS - 1 :]
+    def spare_row(c, i, carry):
+        d = lane_at(c, i)
+        wide[pl.ds(d, 1), :] = p_recv[d].astype(F32)[ROWS - 1 :]
         return carry
 
-    lax.fori_loop(0, peers, spare_row, 0, unroll=8)
+    for c, f in groups:
+        wait_group((c, f), p_recv, 2)
+        for i in range(f, f + batch):
+            spare_row(c, i, 0)
     tags = tagc[...]
     line = wide[...]
     middle, low = pltpu.roll(line, HD - ROWS, 1), pltpu.roll(line, HD - 2 * ROWS, 1)
@@ -385,28 +439,25 @@
         den_s[pl.ds(s, 1), :] = jnp.sum(mine_s, axis=0, keepdims=True)
     new_weight = jnp.exp(new_peak - top)
     inverse = 1.0 / (den_s[...] + new_total * new_weight)
-    den_s[...] = inverse
-    lane_inv = jnp.zeros((peers, HD), F32)
-    for s in range(slots):
-        lane_inv = jnp.where(tags == float(s), den_s[pl.ds(s, 1), :], lane_inv)
-    wide[...] = weight * lane_inv
-    new_share = new_weight * inverse
-
+    wide[...] = weight
     on_row = iota((ROWS, HD), 0) == iota((ROWS, HD), 1)
 
-    def weigh(l, carry):
-        row = jnp.where(on_row, wide[pl.ds(l, 1), :], 0.0)
+    def weigh(c, i, carry):
+        d = lane_at(c, i)
+        row = jnp.where(on_row, wide[pl.ds(d, 1), :], 0.0)
         column = jnp.sum(row, axis=1, keepdims=True)
-        at = pl.ds(pl.multiple_of(l * ROWS, ROWS), ROWS)
-        weighted[at, :] = (p_recv[l].astype(F32) * column).astype(BF16)
+        at = pl.ds(pl.multiple_of((c * plane + i) * ROWS, ROWS), ROWS)
+        weighted[at, :] = (p_recv[d].astype(F32) * column).astype(BF16)
         return carry
 
-    lax.fori_loop(0, peers, weigh, 0, unroll=8)
+    for c in range(side):
+        lax.fori_loop(0, plane, functools.partial(weigh, c), 0, unroll=16)
     mixed = jnp.dot(sel_t[...], weighted[...], preferred_element_type=F32)
     for r in range(rows):
         t, g = r // group, r % group
         at = slice(r * slots, (r + 1) * slots)
-        res = mixed[at] + new_share[:, r : r + 1] * new_mixed[at, :]
+        res = mixed[at] + new_weight[:, r : r + 1] * new_mixed[at, :]
+        res = res * inverse[:, r : r + 1]
         out_ref[t, :, g * HD : (g + 1) * HD] = res.astype(BF16)
 
     @pl.when(is_inner)
@@ -447,16 +498,18 @@
     chunk = width // ranks
     dims = (steps, slots, chunk, pool, block_len, group)
     hbm = pl.BlockSpec(memory_space=pltpu.HBM)
-    smem = pl.BlockSpec(memory_space=pltpu.SMEM)
     vmem = pltpu.VMEM
     dma = pltpu.SemaphoreType.DMA
     return pl.pallas_call(
         functools.partial(kernel, peers, ranks, dims),
         out_shape=jax.ShapeDtypeStruct(query_base_rows.shape, BF16),
-        in_specs=[hbm] * 6 + [smem] * 3 + [hbm] * 4,
+        in_specs=[hbm] * 13,
         out_specs=pl.BlockSpec(memory_space=pltpu.VMEM),
         scratch_shapes=[
             vmem((steps, slots, chunk), BF16),
+            pltpu.SMEM(block_dest.shape, jnp.int32),
+            pltpu.SMEM(block_slot.shape, jnp.int32),
+            pltpu.SMEM(block_fill.shape, jnp.int32),
             vmem(query_base_rows.shape, BF16),
             vmem(k_base.shape, BF16),
             vmem(value_base_rows.shape, BF16),
@@ -476,7 +529,6 @@
             vmem((ROWS * slots, peers * ROWS), BF16),
             vmem((peers, ROWS, HD), BF16),
             vmem((peers, ROWS, HD), BF16),
-            vmem((pool, ROWS, HD), BF16),
             vmem((peers, ROWS, HD), BF16),
             vmem((peers, ROWS, HD), BF16),
             vmem((ROWS * slots, HD), F32),
@@ -484,10 +536,11 @@
             vmem((slots, HD), F32),
             vmem((peers, HD), F32),
             vmem((peers * ROWS, HD), BF16),
-            dma((10,)),
+            dma((13,)),
             dma,
             dma((3,)),
-            dma((3,)),
+            dma((1,)),
+            dma((2, 8)),
             dma((2,)),
             dma((2,)),
             pltpu.SemaphoreType.REGULAR,

time: 44.4 us -> 42 us (0.946)
  the two profiles are of different devices: /device:TPU:24 before, /device:TPU:1 now
where the time goes in v3:
time: 42 us; the launch traced here: 41.8 us
  Pallas kernels  40.3 us (96%)
  local copies, waits for them, and re-layouts  1.46 us (3%)
    pallas_call x1, Pallas kernels, on_device(): pl.pallas_call(functools.partial(kernel, peers, ranks, dims), out_shape=j...  40.3 us
    unnamed x1, local copies, waits for them, and re-layouts  1.46 us

profile of v3, /device:TPU:1, one launch (start us, length us, event | category | flops | bytes accessed | tf_op | source)
XLA Modules:
  0.0 41.8 jit_solution(3554127717748534678)
XLA Ops:
  0.0 40.3 %shard_map.127 = bf16[3,16,640]{2,1,0:T(8,128)(2,1)} custom-call(bf16[3,16,5120]{2,1,0:T(8,128)(2,1)} %x_hbm.1, bf16[3,16,640]{2,1,0:T(8,128)(2,1)} %qb_hbm.1, bf16[3,16,128]{2,1,0:T(8,128)(2,1)} %kb_hbm.1, bf16[3,16,128]{2,1,0:T(8,128)(2,1)} %vb_hbm.1, bf16[32,128,128]{2,1,0:T(8,128)(2,1)} %kp_hbm.1, bf16[32,128,128]{2,1,0:T(8,128)(2,1)} %vp_hbm.1, ...), custom_call_target="tpu_custom_call" | custom-call | tf_op jit(solution)/shard_map/pallas_call | solution.py:503
  40.3 1.5 %copy.15 = bf16[3,16,640]{2,1,0:T(8,128)(2,1)} copy(bf16[3,16,640]{2,1,0:T(8,128)(2,1)} %shard_map.127) | data formatting | bytes 122880

commit v4 on v3

--- a/solution.py
+++ b/solution.py
@@ -103,12 +103,12 @@
     chips = ranks // 2
     chip, core = ml // 2, lax.rem(ml, 2)
     partner = ml + 1 - 2 * core
-    is_inner, is_outer = chip < 2, chip >= 2
+    is_inner, is_outer = chip == 0, chip > 0
     is_outer0 = jnp.logical_and(is_outer, core == 0)
     is_outer1 = jnp.logical_and(is_outer, core == 1)
-    n_inner = 4
+    n_inner = 2
     barrier = pltpu.get_barrier_semaphore()
-    gatherer = ml - core * (chip // 2)
+    gatherer = ml - core * ((chip + chips - 1) // chips)
 
     start = pl.multiple_of(ml * chunk, HD)
     pairs = [
@@ -141,9 +141,7 @@
 
     @pl.when(is_inner)
     def _():
-        signal(barrier, me, 2 - 2 * chip)
-        signal(barrier, me, 3 - 2 * chip)
-        for j in range(2, chips):
+        for j in range(1, chips):
             signal(barrier, me, 2 * j + 1)
 
     @pl.when(is_inner)
@@ -153,15 +151,26 @@
     for load in loads[3:]:
         load.start()
 
-    for load in loads[:3]:
-        load.wait()
-    partial = lax.dot_general(
-        x[...].reshape(steps * slots, chunk),
-        a_both[...],
-        (((1,), (1,)), ((), ())),
-        preferred_element_type=F32,
-    )
-    low_recv[ml] = partial.astype(BF16)
+    half = steps * slots // 2
+    urgent = 2 * ROWS
+
+    def packed(low):
+        return jnp.concatenate([low[:half], low[half:]], axis=1)
+
+    def unpacked(low):
+        return jnp.concatenate([low[:, :rank], low[:, rank:]], axis=0).astype(BF16)
+
+    def make_partial():
+        for load in loads[:3]:
+            load.wait()
+        partial = lax.dot_general(
+            x[...].reshape(steps * slots, chunk),
+            a_both[...],
+            (((1,), (1,)), ((), ())),
+            preferred_element_type=F32,
+        )
+        both = jnp.concatenate([packed(partial[:, :rank]), packed(partial[:, rank:])], axis=0)
+        low_recv[ml] = both.astype(BF16)
 
     def to_learn(src, dst, k, learn):
         return pltpu.make_async_remote_copy(
@@ -173,9 +182,16 @@
             device_id_type=MESH,
         )
 
-    @pl.when(is_inner)
-    def _():
-        pl.semaphore_wait(barrier, peers + 2)
+    low_parts = [pl.ds(0, urgent), pl.ds(urgent, steps * slots - urgent)]
+
+    def send_partial(k, targets):
+        mine = low_recv.at[ml, low_parts[k]]
+        for target in targets:
+            to_learn(mine, mine, k, target).start()
+
+    @pl.when(is_outer)
+    def _():
+        make_partial()
 
     @pl.when(is_outer1)
     def _():
@@ -186,21 +202,9 @@
     def _():
         pl.semaphore_wait(inner_in, 1)
 
-    my_low = low_recv.at[ml]
-
-    @pl.when(is_inner)
-    def _():
-        to_learn(my_low, my_low, 0, partner).start()
-        to_learn(my_low, my_low, 0, 2 - 2 * chip).start()
-        to_learn(my_low, my_low, 0, 3 - 2 * chip).start()
-
     @pl.when(is_outer)
     def _():
-        for j in range(n_inner):
-            to_learn(my_low, my_low, 0, j).start()
-
-    @pl.when(is_outer)
-    def _():
+        send_partial(0, range(n_inner))
         lax.fori_loop(1, peers, greet, 0, unroll=7)
 
     for load in loads[10:12]:
@@ -218,6 +222,11 @@
     to_smem = pltpu.make_async_copy(lane_vec, lane_blk, blk_sem)
     to_smem.start()
 
+    @pl.when(is_inner)
+    def _():
+        make_partial()
+        pl.semaphore_wait(barrier, peers)
+
     @pl.when(is_outer0)
     def _():
         pl.semaphore_wait(barrier, 2 * peers - 1)
@@ -288,6 +297,15 @@
     to_roll(lambda d: tag_send, tag_recv.at[pl.ds(me, 1), :], 0)
 
 
+    @pl.when(is_inner)
+    def _():
+        send_partial(0, [partner])
+        send_partial(1, [partner])
+
+    @pl.when(is_outer)
+    def _():
+        send_partial(1, range(n_inner))
+
     def wait_lanes(buf, sem):
         pltpu.make_async_copy(buf.at[others], buf.at[others], sem).wait()
 
@@ -316,18 +334,27 @@
     for load in loads[3:5]:
         load.wait()
 
-    @pl.when(is_inner)
-    def _():
-        wait_for(low_recv.at[pl.ds(0, ranks - 1)], low_recv_sem.at[0])
-        summed = functools.reduce(jnp.add, [low_recv[j].astype(F32) for j in range(ranks)])
-        low_total[...] = summed.astype(BF16)
-        to_learn(low_total, low_total, 1, 2 * (chips - 1 - chip) + core).start()
-
-    @pl.when(is_outer)
-    def _():
-        wait_for(low_total, low_recv_sem.at[1])
-
-    up = jnp.dot(low_total[:, :rank], qu[...], preferred_element_type=F32)
+    def sum_part(k):
+        at = low_parts[k]
+
+        @pl.when(is_inner)
+        def _():
+            wait_for(low_recv.at[pl.ds(0, ranks - 1), at], low_recv_sem.at[k])
+            summed = functools.reduce(
+                jnp.add, [low_recv[j, at, :].astype(F32) for j in range(ranks)]
+            )
+            low_total[at, :] = summed.astype(BF16)
+            total = low_total.at[at]
+            for j in range(1, chips):
+                to_learn(total, total, k + 2, 2 * j + core).start()
+
+        @pl.when(is_outer)
+        def _():
+            wait_for(low_total.at[at], low_recv_sem.at[k + 2])
+
+    sum_part(0)
+    low_q = unpacked(low_total[:urgent, :].astype(F32)[:half])
+    up = jnp.dot(low_q, qu[...], preferred_element_type=F32)
     query = qb[...].reshape(steps * slots, group * HD).astype(F32) + adapter_scale * up
     query = query.astype(BF16)
     tiles = [
@@ -344,6 +371,7 @@
             to_group((c, f), q_send, q_recv, 1)
     q_recv[me] = q_send[0]
 
+    sum_part(1)
     sel_t[...] = sel[...].T
 
     for load in loads[8:10] + loads[12:]:
@@ -388,7 +416,8 @@
 
     for load in loads[5:8]:
         load.wait()
-    up_v = jnp.dot(low_total[:, rank:], vu[...], preferred_element_type=F32)
+    low_v = unpacked(low_total[...].astype(F32)[half:])
+    up_v = jnp.dot(low_v, vu[...], preferred_element_type=F32)
     value = vb[...].reshape(steps * slots, HD).astype(F32) + adapter_scale * up_v
     value = value.astype(BF16).astype(F32)
     values = [value[t * slots : (t + 1) * slots] for t in range(steps)]
@@ -462,12 +491,14 @@
 
     @pl.when(is_inner)
     def _():
-        wait_for(low_recv.at[pl.ds(0, n_inner - 1)], low_send_sem.at[0])
-        wait_for(low_total, low_send_sem.at[1])
+        for k in range(2):
+            wait_for(low_recv.at[0, low_parts[k]], low_send_sem.at[k])
+            wait_for(low_recv.at[pl.ds(0, chips - 1), low_parts[k]], low_send_sem.at[k + 2])
 
     @pl.when(is_outer)
     def _():
-        wait_for(low_recv.at[pl.ds(0, n_inner)], low_send_sem.at[0])
+        for k in range(2):
+            wait_for(low_recv.at[pl.ds(0, n_inner), low_parts[k]], low_send_sem.at[k])
 
     wait_lanes(tag_recv, send_sem.at[0])
     wait_lanes(q_recv, send_sem.at[1])
@@ -541,8 +572,8 @@
             dma((3,)),
             dma((1,)),
             dma((2, 8)),
-            dma((2,)),
-            dma((2,)),
+            dma((4,)),
+            dma((4,)),
             pltpu.SemaphoreType.REGULAR,
             pltpu.SemaphoreType.REGULAR,
         ],

time: 42 us -> 41 us (0.976)
  the two profiles are of different devices: /device:TPU:1 before, /device:TPU:128 now
where the time goes in v4:
time: 41 us; the launch traced here: 40.8 us
  Pallas kernels  39.4 us (96%)
  local copies, waits for them, and re-layouts  1.46 us (4%)
    pallas_call x1, Pallas kernels, on_device(): pl.pallas_call(functools.partial(kernel, peers, ranks, dims), out_shape=j...  39.4 us
    unnamed x1, local copies, waits for them, and re-layouts  1.46 us

profile of v4, /device:TPU:128, one launch (start us, length us, event | category | flops | bytes accessed | tf_op | source)
XLA Modules:
  0.0 40.8 jit_solution(10893006425982536538)
XLA Ops:
  0.0 39.4 %shard_map.127 = bf16[3,16,640]{2,1,0:T(8,128)(2,1)} custom-call(bf16[3,16,5120]{2,1,0:T(8,128)(2,1)} %x_hbm.1, bf16[3,16,640]{2,1,0:T(8,128)(2,1)} %qb_hbm.1, bf16[3,16,128]{2,1,0:T(8,128)(2,1)} %kb_hbm.1, bf16[3,16,128]{2,1,0:T(8,128)(2,1)} %vb_hbm.1, bf16[32,128,128]{2,1,0:T(8,128)(2,1)} %kp_hbm.1, bf16[32,128,128]{2,1,0:T(8,128)(2,1)} %vp_hbm.1, ...), custom_call_target="tpu_custom_call" | custom-call | tf_op jit(solution)/shard_map/pallas_call | solution.py:534
  39.4 1.5 %copy.15 = bf16[3,16,640]{2,1,0:T(8,128)(2,1)} copy(bf16[3,16,640]{2,1,0:T(8,128)(2,1)} %shard_map.127) | data formatting | bytes 122880

commit v5 on v4

--- a/solution.py
+++ b/solution.py
@@ -256,13 +256,13 @@
     my_y, my_z, my_x = me // plane, lax.rem(me // side, side), lax.rem(me, side)
     z_of = [my_z, my_z + 1 - 2 * lax.rem(my_z, 2), lax.rem(my_z + 2, side), side - 1 - my_z]
 
+    y_at = [lax.rem(my_y + k, side) * plane for k in range(side)]
+    z_at = [z * side for z in z_of]
+    x_at = [lax.rem(my_x + k, side) for k in range(side)]
+
     def lane_at(c, i):
-        over = lax.rem(2 * (i // side), side) + i // (2 * side)
-        return (
-            lax.rem(my_y + over, side) * plane
-            + z_of[c] * side
-            + lax.rem(my_x + lax.rem(i, side), side)
-        )
+        over = 2 * (i // side) % side + i // (2 * side)
+        return y_at[over] + z_at[c] + x_at[i % side]
 
     batch = 8
     groups = [(c, f) for c in range(side) for f in range(0, plane, batch)]
@@ -275,7 +275,7 @@
         c, f = group
         n = (c * plane + f) // batch
 
-        def one(j, carry):
+        for j in range(int(n == 0), batch):
             d = lane_at(c, f + j)
             pltpu.make_async_remote_copy(
                 src_ref=src.at[n * batch + j],
@@ -285,9 +285,6 @@
                 device_id=(d, ml),
                 device_id_type=MESH,
             ).start()
-            return carry
-
-        lax.fori_loop(int(n == 0), batch, one, 0)
 
     def wait_group(group, buf, k):
         c, f = group
@@ -321,15 +318,15 @@
     sel_row = (iota((ROWS, width), 0) * slots).astype(F32)
     sel_lane = iota((ROWS, width), 1).astype(F32)
 
-    def pick(c, i, carry):
+    def pick(c, i):
         row = tagc[pl.ds(lane_at(c, i), 1), :]
         want = sel_row + jnp.concatenate([row] * (width // HD), axis=1)
         hot = jnp.where(want == sel_lane, 1.0, 0.0).astype(BF16)
-        sel[pl.ds(pl.multiple_of((c * plane + i) * ROWS, ROWS), ROWS), :] = hot
-        return carry
+        sel[pl.ds((c * plane + i) * ROWS, ROWS), :] = hot
 
     for c in range(side):
-        lax.fori_loop(0, plane, functools.partial(pick, c), 0, unroll=8)
+        for i in range(plane):
+            pick(c, i)
 
     for load in loads[3:5]:
         load.wait()
@@ -441,15 +438,14 @@
             acc = acc + rounded[u][:, r : r + 1] * values[u]
         new_mixed[pl.ds(r * slots, slots), :] = acc
 
-    def spare_row(c, i, carry):
+    def spare_row(c, i):
         d = lane_at(c, i)
         wide[pl.ds(d, 1), :] = p_recv[d].astype(F32)[ROWS - 1 :]
-        return carry
 
     for c, f in groups:
         wait_group((c, f), p_recv, 2)
         for i in range(f, f + batch):
-            spare_row(c, i, 0)
+            spare_row(c, i)
     tags = tagc[...]
     line = wide[...]
     middle, low = pltpu.roll(line, HD - ROWS, 1), pltpu.roll(line, HD - 2 * ROWS, 1)
@@ -471,16 +467,16 @@
     wide[...] = weight
     on_row = iota((ROWS, HD), 0) == iota((ROWS, HD), 1)
 
-    def weigh(c, i, carry):
+    def weigh(c, i):
         d = lane_at(c, i)
         row = jnp.where(on_row, wide[pl.ds(d, 1), :], 0.0)
         column = jnp.sum(row, axis=1, keepdims=True)
-        at = pl.ds(pl.multiple_of((c * plane + i) * ROWS, ROWS), ROWS)
+        at = pl.ds((c * plane + i) * ROWS, ROWS)
         weighted[at, :] = (p_recv[d].astype(F32) * column).astype(BF16)
-        return carry
 
     for c in range(side):
-        lax.fori_loop(0, plane, functools.partial(weigh, c), 0, unroll=16)
+        for i in range(plane):
+            weigh(c, i)
     mixed = jnp.dot(sel_t[...], weighted[...], preferred_element_type=F32)
     for r in range(rows):
         t, g = r // group, r % group

time: 41 us -> 40.2 us (0.980)
  Pallas kernels: 39.4 us -> 38.6 us
    pallas_call x1, Pallas kernels: 39.4 us -> 38.6 us  [on_device(): pl.pallas_call(functools.partial(kernel, peers, ranks, dims), out_shape=j...]
where the time goes in v5:
time: 40.2 us; the launch traced here: 40 us
  Pallas kernels  38.6 us (96%)
  local copies, waits for them, and re-layouts  1.46 us (4%)
    pallas_call x1, Pallas kernels, on_device(): pl.pallas_call(functools.partial(kernel, peers, ranks, dims), out_shape=j...  38.6 us
    unnamed x1, local copies, waits for them, and re-layouts  1.46 us

profile of v5, /device:TPU:128, one launch (start us, length us, event | category | flops | bytes accessed | tf_op | source)
XLA Modules:
  0.0 40.0 jit_solution(8928563150674168022)
XLA Ops:
  0.0 38.6 %shard_map.127 = bf16[3,16,640]{2,1,0:T(8,128)(2,1)} custom-call(bf16[3,16,5120]{2,1,0:T(8,128)(2,1)} %x_hbm.1, bf16[3,16,640]{2,1,0:T(8,128)(2,1)} %qb_hbm.1, bf16[3,16,128]{2,1,0:T(8,128)(2,1)} %kb_hbm.1, bf16[3,16,128]{2,1,0:T(8,128)(2,1)} %vb_hbm.1, bf16[32,128,128]{2,1,0:T(8,128)(2,1)} %kp_hbm.1, bf16[32,128,128]{2,1,0:T(8,128)(2,1)} %vp_hbm.1, ...), custom_call_target="tpu_custom_call" | custom-call | tf_op jit(solution)/shard_map/pallas_call | solution.py:530
  38.6 1.5 %copy.15 = bf16[3,16,640]{2,1,0:T(8,128)(2,1)} copy(bf16[3,16,640]{2,1,0:T(8,128)(2,1)} %shard_map.127) | data formatting | bytes 122880

commit v6 on v5

--- a/solution.py
+++ b/solution.py
@@ -527,9 +527,24 @@
     hbm = pl.BlockSpec(memory_space=pltpu.HBM)
     vmem = pltpu.VMEM
     dma = pltpu.SemaphoreType.DMA
+    arrays = (
+        x_rows,
+        query_base_rows,
+        k_base,
+        value_base_rows,
+        k_pool,
+        v_pool,
+        block_dest,
+        block_slot,
+        block_fill,
+        a_query,
+        query_up_factor,
+        a_value,
+        value_up_factor,
+    )
     return pl.pallas_call(
         functools.partial(kernel, peers, ranks, dims),
-        out_shape=jax.ShapeDtypeStruct(query_base_rows.shape, BF16),
+        out_shape=pltpu.VMEM(query_base_rows.shape, BF16),
         in_specs=[hbm] * 13,
         out_specs=pl.BlockSpec(memory_space=pltpu.VMEM),
         scratch_shapes=[
@@ -574,23 +589,9 @@
             pltpu.SemaphoreType.REGULAR,
         ],
         compiler_params=pltpu.CompilerParams(
-            collective_id=0, has_side_effects=True, vmem_limit_bytes=64 * 1024 * 1024
+            collective_id=0, has_side_effects=True, vmem_limit_bytes=48 * 1024 * 1024
         ),
-    )(
-        x_rows,
-        query_base_rows,
-        k_base,
-        value_base_rows,
-        k_pool,
-        v_pool,
-        block_dest,
-        block_slot,
-        block_fill,
-        a_query,
-        query_up_factor,
-        a_value,
-        value_up_factor,
-    )
+    )(*[pltpu.with_memory_space_constraint(array, pltpu.HBM) for array in arrays])
 
 
 def solution(mesh):

time: 40.2 us -> 38.7 us (0.963)
  local copies, waits for them, and re-layouts: 1.46 us -> 0.63 us
  Pallas kernels: 38.6 us -> 37.9 us
    unnamed x1, local copies, waits for them, and re-layouts: 1.46 us -> 0.63 us
    pallas_call x1, Pallas kernels: 38.6 us -> 37.9 us  [on_device(): pl.pallas_call(functools.partial(kernel, peers, ranks, dims), out_shape=p...]
where the time goes in v6:
time: 38.7 us; the launch traced here: 38.6 us
  Pallas kernels  37.9 us (98%)
  local copies, waits for them, and re-layouts  0.63 us (2%)
    pallas_call x1, Pallas kernels, on_device(): pl.pallas_call(functools.partial(kernel, peers, ranks, dims), out_shape=p...  37.9 us

profile of v6, /device:TPU:128, one launch (start us, length us, event | category | flops | bytes accessed | tf_op | source)
XLA Modules:
  0.0 38.6 jit_solution(13713622978515946095)
XLA Ops:
  0.0 37.9 %shard_map.127 = bf16[3,16,640]{2,1,0:T(8,128)(2,1)S(1)} custom-call(bf16[3,16,5120]{2,1,0:T(8,128)(2,1)} %x_hbm.1, bf16[3,16,640]{2,1,0:T(8,128)(2,1)} %qb_hbm.1, bf16[3,16,128]{2,1,0:T(8,128)(2,1)} %kb_hbm.1, bf16[3,16,128]{2,1,0:T(8,128)(2,1)} %vb_hbm.1, bf16[32,128,128]{2,1,0:T(8,128)(2,1)} %kp_hbm.1, bf16[32,128,128]{2,1,0:T(8,128)(2,1)} %vp_hbm.1, ...), custom_call_target="tpu_custom_call" | custom-call | tf_op jit(solution)/shard_map/pallas_call | solution.py:545
  37.9 0.6 %copy.15 = bf16[3,16,640]{2,1,0:T(8,128)(2,1)} copy(bf16[3,16,640]{2,1,0:T(8,128)(2,1)S(1)} %shard_map.127) | data formatting | bytes 122880

commit v7 on v6

--- a/solution.py
+++ b/solution.py
@@ -345,11 +345,13 @@
             for j in range(1, chips):
                 to_learn(total, total, k + 2, 2 * j + core).start()
 
+    def take_part(k):
         @pl.when(is_outer)
         def _():
-            wait_for(low_total.at[at], low_recv_sem.at[k + 2])
+            wait_for(low_total.at[low_parts[k]], low_recv_sem.at[k + 2])
 
     sum_part(0)
+    take_part(0)
     low_q = unpacked(low_total[:urgent, :].astype(F32)[:half])
     up = jnp.dot(low_q, qu[...], preferred_element_type=F32)
     query = qb[...].reshape(steps * slots, group * HD).astype(F32) + adapter_scale * up
@@ -368,7 +370,6 @@
             to_group((c, f), q_send, q_recv, 1)
     q_recv[me] = q_send[0]
 
-    sum_part(1)
     sel_t[...] = sel[...].T
 
     for load in loads[8:10] + loads[12:]:
@@ -409,10 +410,13 @@
         wait_group(lanes_group, q_recv, 1)
         some_lanes(lanes_group)
         to_group(lanes_group, p_send, p_recv, 2)
+        if lanes_group == (1, batch):
+            sum_part(1)
     p_recv[me] = p_send[0]
 
     for load in loads[5:8]:
         load.wait()
+    take_part(1)
     low_v = unpacked(low_total[...].astype(F32)[half:])
     up_v = jnp.dot(low_v, vu[...], preferred_element_type=F32)
     value = vb[...].reshape(steps * slots, HD).astype(F32) + adapter_scale * up_v

time: 38.7 us -> 38.5 us (level)
  no operation moved by 1% of the time
where the time goes in v7:
time: 38.5 us; the launch traced here: 38.3 us
  Pallas kernels  37.7 us (98%)
  local copies, waits for them, and re-layouts  0.63 us (2%)
    pallas_call x1, Pallas kernels, on_device(): pl.pallas_call(functools.partial(kernel, peers, ranks, dims), out_shape=p...  37.7 us

profile of v7, /device:TPU:128, one launch (start us, length us, event | category | flops | bytes accessed | tf_op | source)
XLA Modules:
  0.0 38.3 jit_solution(8480350834673355688)
XLA Ops:
  0.0 37.7 %shard_map.127 = bf16[3,16,640]{2,1,0:T(8,128)(2,1)S(1)} custom-call(bf16[3,16,5120]{2,1,0:T(8,128)(2,1)} %x_hbm.1, bf16[3,16,640]{2,1,0:T(8,128)(2,1)} %qb_hbm.1, bf16[3,16,128]{2,1,0:T(8,128)(2,1)} %kb_hbm.1, bf16[3,16,128]{2,1,0:T(8,128)(2,1)} %vb_hbm.1, bf16[32,128,128]{2,1,0:T(8,128)(2,1)} %kp_hbm.1, bf16[32,128,128]{2,1,0:T(8,128)(2,1)} %vp_hbm.1, ...), custom_call_target="tpu_custom_call" | custom-call | tf_op jit(solution)/shard_map/pallas_call | solution.py:549
  37.7 0.6 %copy.15 = bf16[3,16,640]{2,1,0:T(8,128)(2,1)} copy(bf16[3,16,640]{2,1,0:T(8,128)(2,1)S(1)} %shard_map.127) | data formatting | bytes 122880
